TPU v7x, 32 devices: a whole 2x2x4 slice. The times are simulated.
32 devices in a mesh: cluster: 4 (over y, x), sub: 8 (over z, core).
Axes of the slice: x: 2, y: 2, z: 4, core: 2. Of those that a mesh axis runs over, the one named last changes fastest.
Arguments:
- dual_ops: float32 [32768, 1024], P(('cluster', 'sub')), may hold values from -21 to 21, as said below
- boundary_solve_blocks: float32 [32768, 1024], P(('cluster', 'sub')), may hold values from -21 to 21, as said below
- rigid_images: float32 [192, 1024], P(('cluster', 'sub')), may hold values from -0.1875 to 0.1875
- coarse_rows: float32 [192, 192], P(('cluster', 'sub')), may hold values from -1.5 to 1.5, as said below
- gap_raw: float32 [32768, 256], P(('cluster', 'sub')), may hold values from -12 to 12
- row_maps: int32 [32, 2, 128], P(('cluster', 'sub')), may hold values from 0 to 1023, as said below
Outputs:
- multipliers: float32 [32768, 256], P(('cluster', 'sub'))
- residual: float32 [32768, 256], P(('cluster', 'sub'))
- norms: float32 [2, 256], replicated
Inputs may be any that keep to these rules, and one draw needn't show every extreme that they name: `row_maps`: A subdomain's 2 * 128 row numbers all differ; its second list faces the first list of the next subdomain, row by row. `dual_ops`: each block of a subdomain is symmetric positive definite. `boundary_solve_blocks`: each block of a subdomain is symmetric positive definite. `coarse_rows`: Symmetric.
All inputs are finite; a program needn't handle non-finite values.
Results may differ from a plain program's by a relative error of at most 0.0003.
Values sent between devices are 32-bit elements; how exact they have to be, the bound alone decides.
A program may use at most 64 MiB of HBM per device.

v0:
```python
import jax
import jax.numpy as jnp
from jax import lax
from jax.sharding import PartitionSpec as P

ITERS = 2


finest_tier = lax.Precision.HIGHEST


def passed_along(value, axis, steps):
    count = lax.axis_size(axis)
    initial, last = (max(0, -steps), min(count, count - steps))
    return lax.ppermute(value, axis, [(source, source + steps) for source in range(initial, last)])


def shards(dual_ops, boundary_solve_blocks, rigid_images, coarse_rows, gap_raw, row_maps):
    processor_count = lax.axis_size(("cluster", "sub"))
    chain_place = lax.axis_index(("cluster", "sub"))
    left_neighbour_rows = row_maps[0, 0]
    right_neighbour_rows = row_maps[0, 1]
    local_rows = gap_raw.shape[0]
    weight = jnp.ones((local_rows,), jnp.float32)
    weight = weight.at[left_neighbour_rows].set(
        jnp.where(chain_place > 0, 0.5, 1.0).astype(jnp.float32)
    )
    weight = weight.at[right_neighbour_rows].set(
        jnp.where(chain_place < processor_count - 1, 0.5, 1.0).astype(jnp.float32)
    )
    interface_weights = weight[:, None]

    def assemble_dual(deformation_vector):
        outgoing_right = deformation_vector[right_neighbour_rows]
        outgoing_left = deformation_vector[left_neighbour_rows]
        from_left = passed_along(outgoing_right, ("cluster", "sub"), 1)
        from_right = passed_along(outgoing_left, ("cluster", "sub"), -1)
        return (
            deformation_vector.at[left_neighbour_rows]
            .add(from_left)
            .at[right_neighbour_rows]
            .add(from_right)
        )

    def gather_onto_subdomain_vector(back_rows):
        outgoing_right = back_rows[right_neighbour_rows]
        outgoing_left = back_rows[left_neighbour_rows]
        from_left = passed_along(outgoing_right, ("cluster", "sub"), 1)
        from_right = passed_along(outgoing_left, ("cluster", "sub"), -1)
        return (
            back_rows.at[left_neighbour_rows]
            .add(from_left)
            .at[right_neighbour_rows]
            .add(from_right)
        )

    def coarse_fold(piece):
        return jnp.dot(
            coarse_rows, piece, precision=finest_tier, preferred_element_type=jnp.float32
        )

    def project(deformation_vector, partial_value):
        kernel_basis_matrix = jnp.dot(
            rigid_images,
            deformation_vector,
            precision=finest_tier,
            preferred_element_type=jnp.float32,
        )
        nearby = lax.all_gather(kernel_basis_matrix, "sub", axis=0, tiled=True)
        load_amounts = coarse_fold(lax.all_gather(nearby, "cluster", axis=0, tiled=True))
        total = lax.psum(partial_value, ("cluster", "sub"))
        back_rows = jnp.einsum("km,kr->mr", rigid_images, load_amounts, precision=finest_tier)
        return (deformation_vector - gather_onto_subdomain_vector(back_rows), total)

    residual = assemble_dual(gap_raw)
    multipliers = jnp.zeros_like(gap_raw)
    search_direction = multipliers
    previous_norm = jnp.ones((gap_raw.shape[1],), jnp.float32)
    norm_list = []
    for iteration in range(ITERS):
        norm_part = jnp.sum(interface_weights * residual * residual, axis=0)
        projected_residual, squared_length_sum = project(residual, norm_part)
        norm_list.append(squared_length_sum)
        local_contributions = jnp.dot(
            boundary_solve_blocks,
            interface_weights * projected_residual,
            precision=finest_tier,
            preferred_element_type=jnp.float32,
        )
        smoothed = interface_weights * assemble_dual(local_contributions)
        precond_part = jnp.sum(interface_weights * projected_residual * smoothed, axis=0)
        update, precond_norm = project(smoothed, precond_part)
        if iteration == 0:
            search_direction = update
        else:
            search_direction = update + precond_norm / previous_norm * search_direction
        rigid_image = assemble_dual(
            jnp.dot(
                dual_ops,
                search_direction,
                precision=finest_tier,
                preferred_element_type=jnp.float32,
            )
        )
        bending = lax.psum(
            jnp.sum(interface_weights * search_direction * rigid_image, axis=0), ("cluster", "sub")
        )
        step_size = precond_norm / bending
        multipliers = multipliers + step_size * search_direction
        residual = residual - step_size * rigid_image
        previous_norm = precond_norm
    return (multipliers, residual, jnp.stack(norm_list))


def solution(mesh):
    in_specs = (
        P(("cluster", "sub"), None),
        P(("cluster", "sub"), None),
        P(("cluster", "sub"), None),
        P(("cluster", "sub"), None),
        P(("cluster", "sub"), None),
        P(("cluster", "sub"), None, None),
    )
    out_specs = (P(("cluster", "sub"), None), P(("cluster", "sub"), None), P())
    return jax.shard_map(shards, mesh=mesh, in_specs=in_specs, out_specs=out_specs, check_vma=False)
```

profile of v0, /device:TPU:0, one launch (start us, length us, event | category | flops | bytes accessed | tf_op | source)
XLA Modules:
  0.0 434.5 jit_solution(2825295080090032864)
XLA Ops:
  3.4 2.4 collective-permute-start
  7.9 1.7 scatter_fusion.1
  9.5 2.4 collective-permute-done.1
  14.3 19.6 %all-gather = f32[8,6,256]{2,1,0:T(8,128)S(1)} all-gather(f32[1,6,256]{2,1,0:T(8,128)S(1)} %convolution_bitcast_fusion.11), channel_id=1, replica_groups=mesh['cluster'=4,'sub'=8] {'sub'}, dimensions={0}, use_global_device_ids=true | all-gather | bytes 55296 | tf_op jit(solution)/shard_map/all_gather | solution.py:69
  33.8 9.6 %all_gather.25 = f32[192,256]{1,0:T(8,128)S(1)} all-gather(f32[48,256]{1,0:T(8,128)S(1)} %reshape.371), channel_id=1, replica_groups=mesh['cluster'=4,'sub'=8] {'cluster'}, dimensions={0}, use_global_device_ids=true | all-gather | bytes 245760 | tf_op jit(solution)/shard_map/all_gather | solution.py:70
  51.2 1.7 scatter_fusion.3
  52.9 2.1 scatter_fusion.4
  55.1 10.3 %convolution_bitcast_fusion.6 = f32[1024,256]{0,1:T(8,128)} fusion(f32[1024,1024]{1,0:T(8,128)} %param.7, f32[1024,256]{1,0:T(8,128)S(1)} %scatter_fusion.2, f32[1024,256]{1,0:T(8,128)S(1)} %scatter_fusion.4, f32[1024]{0:T(1024)S(1)} %scatter_fusion), kind=kOutput, calls=%fused_computation.46 | convolution fusion | flops 3221749760 | bytes 7344128 | tf_op jit(solution)/shard_map/dot_general | solution.py:84
  68.3 3.5 collective-permute-start.4
  74.6 1.7 scatter_fusion.5
  76.7 1.7 scatter_fusion.6
  79.1 23.3 %all-gather.1 = f32[8,6,256]{2,1,0:T(8,128)S(1)} all-gather(f32[1,6,256]{2,1,0:T(8,128)S(1)} %convolution_bitcast_fusion.10), channel_id=1, replica_groups=mesh['cluster'=4,'sub'=8] {'sub'}, dimensions={0}, use_global_device_ids=true | all-gather | bytes 55296 | tf_op jit(solution)/shard_map/all_gather | solution.py:69
  102.4 10.5 %all_gather.27 = f32[192,256]{1,0:T(8,128)S(1)} all-gather(f32[48,256]{1,0:T(8,128)S(1)} %reshape.373), channel_id=1, replica_groups=mesh['cluster'=4,'sub'=8] {'cluster'}, dimensions={0}, use_global_device_ids=true | all-gather | bytes 245760 | tf_op jit(solution)/shard_map/all_gather | solution.py:70
  113.1 2.1 convolution_bitcast_fusion.5
  115.1 2.5 copy.64
  117.7 2.6 gather_fusion.6
  121.7 2.6 gather_fusion.7
  125.7 3.3 scatter_fusion.7
  129.0 3.3 scatter_fusion.8
  134.8 10.3 %convolution_bitcast_fusion.4 = f32[1024,256]{0,1:T(8,128)} fusion(f32[1024,256]{1,0:T(8,128)S(1)} %multiply_subtract_fusion.2, f32[1024,1024]{1,0:T(8,128)} %param.6), kind=kOutput, calls=%fused_computation.44 | convolution fusion | flops 3221225472 | bytes 6291456 | tf_op jit(solution)/shard_map/dot_general | solution.py:98
  145.0 2.5 copy.67
  147.6 2.6 gather_fusion.8
  150.2 3.4 collective-permute-start.8
  153.6 2.6 gather_fusion.9
  157.5 3.3 scatter_fusion.9
  160.9 3.3 scatter_fusion.10
  164.2 2.0 fusion
  166.2 49.1 %all-reduce.1 = (f32[256]{0:T(256)S(1)}, f32[256]{0:T(256)S(1)}) all-reduce(f32[256]{0:T(256)S(1)} %get-tuple-element.4, f32[256]{0:T(256)S(1)} %get-tuple-element.7), channel_id=1, replica_groups=mesh['cluster'=4,'sub'=8] {'cluster','sub'}, use_global_device_ids=true, to_apply=%region_9.10 | all-reduce | flops 512 | bytes 4096 | tf_op jit(solution)/shard_map/psum | solution.py:71
  217.4 14.5 %all-gather.2 = f32[8,6,256]{2,1,0:T(8,128)S(1)} all-gather(f32[1,6,256]{2,1,0:T(8,128)S(1)} %convolution_bitcast_fusion.9), channel_id=1, replica_groups=mesh['cluster'=4,'sub'=8] {'sub'}, dimensions={0}, use_global_device_ids=true | all-gather | bytes 55296 | tf_op jit(solution)/shard_map/all_gather | solution.py:69
  231.9 9.5 %all_gather.29 = f32[192,256]{1,0:T(8,128)S(1)} all-gather(f32[48,256]{1,0:T(8,128)S(1)} %reshape.375), channel_id=1, replica_groups=mesh['cluster'=4,'sub'=8] {'cluster'}, dimensions={0}, use_global_device_ids=true | all-gather | bytes 245760 | tf_op jit(solution)/shard_map/all_gather | solution.py:70
  247.2 1.7 scatter_fusion.11
  249.1 1.7 scatter_fusion.12
  250.8 9.4 %convolution_bitcast_fusion.2 = f32[1024,256]{0,1:T(8,128)S(1)} fusion(f32[1024,1024]{1,0:T(8,128)} %param.7, f32[1024,256]{1,0:T(8,128)S(1)} %multiply_subtract_fusion.1, f32[1024,256]{1,0:T(8,128)S(1)} %scatter_fusion.12, f32[1024]{0:T(1024)S(1)} %scatter_fusion), kind=kOutput, calls=%fused_computation.42 | convolution fusion | flops 3221749760 | bytes 7344128 | tf_op jit(solution)/shard_map/dot_general | solution.py:84
  261.3 5.4 %collective-permute-start.12 = (f32[128,256]{1,0:T(8,128)S(1)}, f32[128,256]{1,0:T(8,128)S(1)}, u32[]{:S(2)}, u32[]{:S(2)}) collective-permute-start(f32[128,256]{1,0:T(8,128)S(1)} %gather_fusion.12), channel_id=1, source_target_pairs={{0,1},{1,2},{2,3},{3,4},{4,5},{5,6},{6,7},{7,8},{8,9},{9,10},{10,1... | collective-permute-start | bytes 393224 | tf_op jit(solution)/shard_map/ppermute | solution.py:15
  268.8 1.7 scatter_fusion.13
  270.7 1.7 scatter_fusion.14
  273.1 22.3 %all-gather.3 = f32[8,6,256]{2,1,0:T(8,128)S(1)} all-gather(f32[1,6,256]{2,1,0:T(8,128)S(1)} %convolution_bitcast_fusion.8), channel_id=1, replica_groups=mesh['cluster'=4,'sub'=8] {'sub'}, dimensions={0}, use_global_device_ids=true | all-gather | bytes 55296 | tf_op jit(solution)/shard_map/all_gather | solution.py:69
  295.4 10.5 %all_gather.31 = f32[192,256]{1,0:T(8,128)S(1)} all-gather(f32[48,256]{1,0:T(8,128)S(1)} %reshape.377), channel_id=1, replica_groups=mesh['cluster'=4,'sub'=8] {'cluster'}, dimensions={0}, use_global_device_ids=true | all-gather | bytes 245760 | tf_op jit(solution)/shard_map/all_gather | solution.py:70
  306.1 2.1 convolution_bitcast_fusion.1
  311.9 1.9 collective-permute-start.14
  316.7 42.0 %psum.44 = f32[256]{0:T(256)S(1)} all-reduce(f32[256]{0:T(256)S(1)} %get-tuple-element.6), channel_id=1, replica_groups=mesh['cluster'=4,'sub'=8] {'cluster','sub'}, use_global_device_ids=true, to_apply=%region_21.22 | all-reduce | flops 256 | bytes 2048 | tf_op jit(solution)/shard_map/psum | solution.py:71
  358.7 2.0 scatter_fusion.15
  360.7 1.7 scatter_fusion.16
  365.0 7.1 %convolution_bitcast_fusion = f32[1024,256]{0,1:T(8,128)S(1)} fusion(f32[1024,256]{1,0:T(8,128)S(1)} %multiply_add_fusion.1, f32[1024,1024]{1,0:T(8,128)S(1)} %copy-done.6), kind=kOutput, calls=%fused_computation.40 | convolution fusion | flops 3221225472 | bytes 6291456 | tf_op jit(solution)/shard_map/dot_general | solution.py:98
  377.8 1.7 scatter_fusion.17
  379.5 3.6 collective-permute-done.17
  386.2 44.6 %all-reduce = (f32[256]{0:T(256)S(1)}, f32[1,256]{1,0:T(1,128)S(1)}, f32[1,256]{1,0:T(1,128)S(1)}) all-reduce(f32[256]{0:T(256)S(1)} %multiply_reduce_fusion, f32[1,256]{1,0:T(1,128)S(1)} %bitcast.73, f32[1,256]{1,0:T(1,128)S(1)} %bitcast.72), channel_id=1, replica_groups=mesh['cluster'=4,'sub'=8] {'cluster','sub'}, use_global_device_ids=true, to_apply=%region_27.28 | all-reduce | flops 768 | bytes 6144 | tf_op jit(solution)/shard_map/psum | solution.py:105
  430.8 2.9 multiply_subtract_fusion
  (100 shorter events, 59.1 us)
Async XLA Ops:
  0.6 13.0 %copy-start = (f32[6,1024]{1,0:T(8,128)S(1)}, f32[6,1024]{1,0:T(8,128)}, u32[]{:S(2)}) copy-start(f32[6,1024]{1,0:T(8,128)} %param.8) | copy-start | bytes 73732
  1.9 41.6 %copy-start.8 = (f32[6,192]{1,0:T(8,128)S(1)}, f32[6,192]{1,0:T(8,128)}, u32[]{:S(2)}) copy-start(f32[6,192]{1,0:T(8,128)} %param.9) | copy-start | bytes 13828
  3.4 4.4 %collective-permute-start = (f32[128,256]{1,0:T(8,128)S(1)}, f32[128,256]{1,0:T(8,128)S(1)}, u32[]{:S(2)}, u32[]{:S(2)}) collective-permute-start(f32[128,256]{1,0:T(8,128)S(1)} %gather_fusion), channel_id=1, source_target_pairs={{0,1},{1,2},{2,3},{3,4},{4,5},{5,6},{6,7},{7,8},{8,9},{9,10},{10,1... | collective-permute-start | bytes 393224 | tf_op jit(solution)/shard_map/ppermute | solution.py:15
  6.5 5.4 %collective-permute-start.1 = (f32[128,256]{1,0:T(8,128)S(1)}, f32[128,256]{1,0:T(8,128)S(1)}, u32[]{:S(2)}, u32[]{:S(2)}) collective-permute-start(f32[128,256]{1,0:T(8,128)S(1)} %gather_fusion.1), channel_id=1, source_target_pairs={{1,0},{2,1},{3,2},{4,3},{5,4},{6,5},{7,6},{8,7},{9,8},{10,9},{11,1... | collective-permute-start | bytes 393224 | tf_op jit(solution)/shard_map/ppermute | solution.py:15
  45.8 5.4 %collective-permute-start.2 = (f32[128,256]{1,0:T(8,128)S(1)}, f32[128,256]{1,0:T(8,128)S(1)}, u32[]{:S(2)}, u32[]{:S(2)}) collective-permute-start(f32[128,256]{1,0:T(8,128)S(1)} %gather_fusion.2), channel_id=1, source_target_pairs={{0,1},{1,2},{2,3},{3,4},{4,5},{5,6},{6,7},{7,8},{8,9},{9,10},{10,1... | collective-permute-start | bytes 393224 | tf_op jit(solution)/shard_map/ppermute | solution.py:15
  47.9 5.0 %collective-permute-start.3 = (f32[128,256]{1,0:T(8,128)S(1)}, f32[128,256]{1,0:T(8,128)S(1)}, u32[]{:S(2)}, u32[]{:S(2)}) collective-permute-start(f32[128,256]{1,0:T(8,128)S(1)} %gather_fusion.3), channel_id=1, source_target_pairs={{1,0},{2,1},{3,2},{4,3},{5,4},{6,5},{7,6},{8,7},{9,8},{10,9},{11,1... | collective-permute-start | bytes 393224 | tf_op jit(solution)/shard_map/ppermute | solution.py:15
  68.3 6.2 %collective-permute-start.4 = (f32[128,256]{1,0:T(8,128)}, f32[128,256]{1,0:T(8,128)S(1)}, u32[]{:S(2)}, u32[]{:S(2)}) collective-permute-start(f32[128,256]{1,0:T(8,128)} %gather_fusion.4), channel_id=1, source_target_pairs={{0,1},{1,2},{2,3},{3,4},{4,5},{5,6},{6,7},{7,8},{8,9},{9,10},{10,1... | collective-permute-start | bytes 393224 | tf_op jit(solution)/shard_map/ppermute | solution.py:15
  73.3 3.4 collective-permute-start.5
  120.3 5.4 %collective-permute-start.6 = (f32[128,256]{1,0:T(8,128)}, f32[128,256]{1,0:T(8,128)S(1)}, u32[]{:S(2)}, u32[]{:S(2)}) collective-permute-start(f32[128,256]{1,0:T(8,128)} %gather_fusion.6), channel_id=1, source_target_pairs={{0,1},{1,2},{2,3},{3,4},{4,5},{5,6},{6,7},{7,8},{8,9},{9,10},{10,1... | collective-permute-start | bytes 393224 | tf_op jit(solution)/shard_map/ppermute | solution.py:15
  124.4 4.6 %collective-permute-start.7 = (f32[128,256]{1,0:T(8,128)}, f32[128,256]{1,0:T(8,128)S(1)}, u32[]{:S(2)}, u32[]{:S(2)}) collective-permute-start(f32[128,256]{1,0:T(8,128)} %gather_fusion.7), channel_id=1, source_target_pairs={{1,0},{2,1},{3,2},{4,3},{5,4},{6,5},{7,6},{8,7},{9,8},{10,9},{11,1... | collective-permute-start | bytes 393224 | tf_op jit(solution)/shard_map/ppermute | solution.py:15
  133.8 1.0 copy-start.3
  150.2 7.3 %collective-permute-start.8 = (f32[128,256]{1,0:T(8,128)}, f32[128,256]{1,0:T(8,128)S(1)}, u32[]{:S(2)}, u32[]{:S(2)}) collective-permute-start(f32[128,256]{1,0:T(8,128)} %gather_fusion.8), channel_id=1, source_target_pairs={{0,1},{1,2},{2,3},{3,4},{4,5},{5,6},{6,7},{7,8},{8,9},{9,10},{10,1... | collective-permute-start | bytes 393224 | tf_op jit(solution)/shard_map/ppermute | solution.py:15
  156.2 4.6 %collective-permute-start.9 = (f32[128,256]{1,0:T(8,128)}, f32[128,256]{1,0:T(8,128)S(1)}, u32[]{:S(2)}, u32[]{:S(2)}) collective-permute-start(f32[128,256]{1,0:T(8,128)} %gather_fusion.9), channel_id=1, source_target_pairs={{1,0},{2,1},{3,2},{4,3},{5,4},{6,5},{7,6},{8,7},{9,8},{10,9},{11,1... | collective-permute-start | bytes 393224 | tf_op jit(solution)/shard_map/ppermute | solution.py:15
  216.7 34.0 %copy-start.1 = (f32[1024,256]{1,0:T(8,128)}, f32[1024,256]{1,0:T(8,128)S(1)}, u32[]{:S(2)}) copy-start(f32[1024,256]{1,0:T(8,128)S(1)} %multiply_subtract_fusion.1) | copy-start | bytes 3145732
  243.8 3.4 collective-permute-start.10
  245.8 3.2 collective-permute-start.11
  261.3 7.5 %collective-permute-start.12 = (f32[128,256]{1,0:T(8,128)S(1)}, f32[128,256]{1,0:T(8,128)S(1)}, u32[]{:S(2)}, u32[]{:S(2)}) collective-permute-start(f32[128,256]{1,0:T(8,128)S(1)} %gather_fusion.12), channel_id=1, source_target_pairs={{0,1},{1,2},{2,3},{3,4},{4,5},{5,6},{6,7},{7,8},{8,9},{9,10},{10,1... | collective-permute-start | bytes 393224 | tf_op jit(solution)/shard_map/ppermute | solution.py:15
  267.5 3.2 collective-permute-start.13
  311.9 46.8 %collective-permute-start.14 = (f32[128,256]{1,0:T(8,128)}, f32[128,256]{1,0:T(8,128)}, u32[]{:S(2)}, u32[]{:S(2)}) collective-permute-start(f32[128,256]{1,0:T(8,128)} %gather_fusion.14), channel_id=1, source_target_pairs={{0,1},{1,2},{2,3},{3,4},{4,5},{5,6},{6,7},{7,8},{8,9},{9,10},{10,1... | collective-permute-start | bytes 393224 | tf_op jit(solution)/shard_map/ppermute | solution.py:15
  313.8 46.9 %collective-permute-start.15 = (f32[128,256]{1,0:T(8,128)S(1)}, f32[128,256]{1,0:T(8,128)S(1)}, u32[]{:S(2)}, u32[]{:S(2)}) collective-permute-start(f32[128,256]{1,0:T(8,128)S(1)} %gather_fusion.15), channel_id=1, source_target_pairs={{1,0},{2,1},{3,2},{4,3},{5,4},{6,5},{7,6},{8,7},{9,8},{10,9},{11,1... | collective-permute-start | bytes 393224 | tf_op jit(solution)/shard_map/ppermute | solution.py:15
  316.7 45.7 %copy-start.4 = (f32[1024,256]{1,0:T(8,128)S(1)}, f32[1024,256]{1,0:T(8,128)}, u32[]{:S(2)}) copy-start(f32[1024,256]{1,0:T(8,128)} %copy-done.3) | copy-start | bytes 3145732
  362.4 2.6 copy-start.6
  362.7 1.0 copy-start.7
  372.4 58.4 %copy-start.2 = (f32[1024,256]{1,0:T(8,128)S(1)}, f32[1024,256]{1,0:T(8,128)}, u32[]{:S(2)}) copy-start(f32[1024,256]{1,0:T(8,128)} %copy-done.1) | copy-start | bytes 3145732
  372.4 58.4 %copy-start.5 = (f32[1024,256]{1,0:T(8,128)S(1)}, f32[1024,256]{1,0:T(8,128)}, u32[]{:S(2)}) copy-start(f32[1024,256]{1,0:T(8,128)} %copy-done.3) | copy-start | bytes 3145732
  373.8 4.0 collective-permute-start.16
  376.5 6.5 %collective-permute-start.17 = (f32[128,256]{1,0:T(8,128)}, f32[128,256]{1,0:T(8,128)S(1)}, u32[]{:S(2)}, u32[]{:S(2)}) collective-permute-start(f32[128,256]{1,0:T(8,128)} %gather_fusion.17), channel_id=1, source_target_pairs={{1,0},{2,1},{3,2},{4,3},{5,4},{6,5},{7,6},{8,7},{9,8},{10,9},{11,1... | collective-permute-start | bytes 393224 | tf_op jit(solution)/shard_map/ppermute | solution.py:15
where the time goes:
time: 442 us; the launch traced here: 435 us
  blocking collectives  255 us (58%)
  other arithmetic  50.1 us (11%)
  matrix products  46.7 us (11%)
  local copies, waits for them, and re-layouts  40.4 us (9%)
  starting transfers between devices  33.5 us (8%)
  waiting for transfers between devices  6.97 us (2%)
    psum x2, blocking collectives, project(): total = lax.psum(partial_value, ('cluster', 'sub'))  91 us
    all_gather x4, blocking collectives, project(): nearby = lax.all_gather(kernel_basis_matrix, 'sub', axis=0, tiled=True)  79.7 us
    psum x1, blocking collectives, shards(): lax.psum(jnp.sum(interface_weights * search_direction * rigid_image, axis...  44.6 us
    all_gather x4, blocking collectives, project(): lax.all_gather(nearby, 'cluster', axis=0, tiled=True)  40 us
    ppermute x18, starting transfers between devices, passed_along(): lax.ppermute(value, axis, [(source, source + steps) for source in range(i...  33.5 us
    scatter-add x10, other arithmetic, assemble_dual(): return deformation_vector.at[left_neighbour_rows].add(from_left).at[right...  20.1 us
    dot_general x2, matrix products, shards(): jnp.dot(boundary_solve_blocks, interface_weights * projected_residual, pr...  19.7 us
    scatter-add x8, other arithmetic, gather_onto_subdomain_vector(): return back_rows.at[left_neighbour_rows].add(from_left).at[right_neighbou...  17.6 us
  transfers between devices with their start and end apart: 18, of which 5 were waited for; matrix products, arithmetic and copies ran while one was open for 8% of the time, Pallas kernels for 0%

commit v1 on v0

v1 whole, which is shorter than its diff:
```python
import functools

import jax
import jax.numpy as jnp
from jax import lax
from jax.experimental import pallas as pl
from jax.experimental.pallas import tpu as pltpu
from jax.sharding import PartitionSpec as P

MESH = pl.DeviceIdType.MESH
PHASES = 5
GROUP = 8
BLOCK = 3 * GROUP
HALF = 128
f32, bf16 = jnp.float32, jnp.bfloat16


def split(x):
    high = x.astype(bf16)
    return high, (x - high.astype(f32)).astype(bf16)


def dot(a, b):
    return jnp.dot(a, b, preferred_element_type=f32)


def dot3(a_high, a_low, b_high, b_low):
    return dot(a_high, b_high) + dot(a_high, b_low) + dot(a_low, b_high)


def each(low, high, body):
    if high - low <= 16:
        for at in range(low, high):
            body(at)
    else:
        lax.fori_loop(low, high, lambda at, carry: (body(at), carry)[1], 0)


def kernel(clusters, subs, dual_hbm, pre_hbm, rigid_ref, coarse_ref, gap_hbm, maps_ref,
           mult_ref, res_ref, norms_ref,
           dual_in, pre_in, dual_h, dual_l, pre_h, pre_l, kd_h, kd_l, kp_h, kp_l,
           gap, place, pick, weight, rx, rxt3, x_h, x_l,
           q0,
           coarse_all, coarse_pick, mix_h, mix_l, rig_out, rig_in,
           one_out, one_in, two_out, two_in, ex_out, ex_in,
           load_sem, rig_ss, rig_rs, co_ss, co_rs, one_ss, one_rs, two_ss, two_rs, ex_ss, ex_rs):
    total = clusters * subs
    modes, m = rigid_ref.shape
    coarse = coarse_ref.shape[1]
    p = maps_ref.shape[2]
    r = gap.shape[1]
    wide = coarse_all.shape[2]
    chunk = m // 4
    c, s = lax.axis_index("cluster"), lax.axis_index("sub")
    me = c * subs + s
    core = lax.rem(s, 2)
    base = s - core
    has_left, has_right = me > 0, me < total - 1
    has = (has_left, has_right)
    left_id = (lax.div(me + total - 1, subs) % clusters, lax.rem(me + total - 1, subs))
    right_id = (lax.div(me + 1, subs) % clusters, lax.rem(me + 1, subs))
    ids = (left_id, right_id)

    r0, p0, u0, y0 = (pre_in.at[:, at * r:(at + 1) * r] for at in range(4))
    im0, g0, tq, y1 = (dual_in.at[:, at * r:(at + 1) * r] for at in range(4))

    loads = []
    for at, (src, dst) in enumerate(((gap_hbm, gap), (pre_hbm, pre_in), (dual_hbm, dual_in))):
        load = pltpu.make_async_copy(src, dst, load_sem.at[at])
        load.start()
        loads.append(load)

    barrier = pltpu.get_barrier_semaphore()

    def greet(device):
        pl.semaphore_signal(barrier, inc=1, device_id=device, device_id_type=MESH)

    def sub_peer(i):
        return lax.rem(s + i, subs)

    def cluster_peer(i):
        return lax.rem(c + i, clusters)

    each(1, subs, lambda i: greet((c, sub_peer(i))))
    for i in range(1, clusters):
        for k in range(2):
            greet((cluster_peer(i), base + k))
    for side in range(2):
        @pl.when(has[side])
        def _():
            greet(ids[side])

    row_list = jnp.concatenate([maps_ref[0, 0:1, :], maps_ref[0, 1:2, :]], axis=1)
    eye = lax.broadcasted_iota(jnp.int32, (2 * p, 2 * p), 0) == lax.broadcasted_iota(
        jnp.int32, (2 * p, 2 * p), 1)
    col_list = jnp.sum(jnp.where(eye, row_list.astype(f32), 0.0), axis=1, keepdims=True)
    pick_f = jnp.where(
        lax.broadcasted_iota(jnp.int32, (2 * p, m), 1).astype(f32) == col_list, 1.0, 0.0)
    pick[...] = pick_f.astype(bf16)
    left_half = jnp.where(has_left, 0.5, 0.0).astype(f32)
    right_half = jnp.where(has_right, 0.5, 0.0).astype(f32)
    row_weight = (1.0 - left_half * jnp.sum(pick_f[:p], axis=0, keepdims=True)
                  - right_half * jnp.sum(pick_f[p:], axis=0, keepdims=True))
    side_half = jnp.where(lax.broadcasted_iota(jnp.int32, (1, 2 * p), 1) < p, left_half, right_half)
    for at in range(0, m, chunk):
        hot = jnp.where(
            lax.broadcasted_iota(jnp.int32, (chunk, 2 * p), 0) + at == row_list, 1.0, 0.0)
        place[at:at + chunk, :] = hot.astype(bf16)
        column = 1.0 - jnp.sum(hot * side_half, axis=1, keepdims=True)
        weight[at:at + chunk, :] = jnp.broadcast_to(column, (chunk, r))

    rx[...] = jnp.zeros_like(rx)
    rx[GROUP:GROUP + modes, :] = rigid_ref[...]
    own_h, own_l = split(rx[GROUP:2 * GROUP, :])
    own_pad = jnp.concatenate([own_h, own_l], axis=0)
    edge = dot(own_pad, place[...])
    edge = edge[:GROUP] + edge[GROUP:]
    rig_out[0] = edge[:, :p]
    rig_out[1] = edge[:, p:]
    coarse_all[me] = jnp.zeros((GROUP, wide), f32)
    coarse_all[me, 0:modes, 0:coarse] = coarse_ref[...]
    for side in range(2):
        @pl.when(jnp.logical_not(has[side]))
        def _():
            rig_in[side] = jnp.zeros((GROUP, p), f32)
            for phase in range(PHASES):
                ex_in[phase, side] = jnp.zeros((p, r), f32)

    pl.semaphore_wait(
        barrier,
        (subs - 1) + 2 * (clusters - 1) + has_left.astype(jnp.int32) + has_right.astype(jnp.int32))

    def remote(src, dst, ss, rs, device):
        return pltpu.make_async_remote_copy(
            src_ref=src, dst_ref=dst, send_sem=ss, recv_sem=rs, device_id=device,
            device_id_type=MESH)

    def rig_copy(side):
        return remote(rig_out.at[side], rig_in.at[1 - side], rig_ss.at[side], rig_rs.at[1 - side],
                      ids[side])

    for side in range(2):
        @pl.when(has[side])
        def _():
            rig_copy(side).start()

    def coarse_copy(i):
        remote(coarse_all.at[me], coarse_all.at[me], co_ss.at[0], co_rs.at[0],
               (c, sub_peer(i))).start()

    each(1, subs, coarse_copy)

    def ex_copy(phase, side):
        return remote(ex_out.at[phase, side], ex_in.at[phase, 1 - side], ex_ss.at[phase, side],
                      ex_rs.at[phase, 1 - side], ids[side])

    def send_edges(phase, edges):
        ex_out[phase, 0] = edges[:p]
        ex_out[phase, 1] = edges[p:2 * p]
        for side in range(2):
            @pl.when(has[side])
            def _():
                ex_copy(phase, side).start()

    def take_edges(phase):
        for side in range(2):
            @pl.when(has[side])
            def _():
                remote(ex_out.at[phase, side], ex_in.at[phase, side], ex_ss.at[phase, side],
                       ex_rs.at[phase, side], ids[side]).wait_recv()
        return split(ex_in[phase].reshape(2 * p, r))

    def send_sums(phase, block, sums):
        rows = lax.broadcasted_iota(jnp.int32, (BLOCK, r), 0)
        for at, value in sums:
            block = jnp.where(rows == at, value, block)
        for k in range(2):
            one_out[phase, k] = block[:, k * HALF:(k + 1) * HALF]
        one_in[phase, s] = one_out[phase, core]

        def go(i):
            peer = sub_peer(i)
            remote(one_out.at[phase, lax.rem(peer, 2)], one_in.at[phase, s], one_ss.at[phase],
                   one_rs.at[phase], (c, peer)).start()

        each(1, subs, go)

    def wait_recv(like, sem):
        remote(like, like, sem, sem, (c, s)).wait_recv()

    def wait_send(like, sem):
        remote(like, like, sem, sem, (c, s)).wait_send()

    def pass_sums(phase):
        wait_recv(one_in.at[phase, pl.ds(0, subs - 1)], one_rs.at[phase])
        b_h, b_l = split(one_in[phase].reshape(subs * BLOCK, HALF))
        part = dot3(mix_h[...], mix_l[...], b_h, b_l)
        two_out[phase] = part.reshape(clusters * 2, BLOCK, HALF)
        two_in[phase, 2 * c + core] = two_out[phase, 2 * c + core]

        def go(to_c, k):
            remote(two_out.at[phase, 2 * to_c + k], two_in.at[phase, 2 * c + core],
                   two_ss.at[phase], two_rs.at[phase], (to_c, base + k)).start()

        for i in range(1, clusters):
            for k in range(2):
                go(cluster_peer(i), k)
        go(c, 1 - core)

    def take_sums(phase):
        wait_recv(two_in.at[phase, pl.ds(0, 2 * clusters - 1)], two_rs.at[phase])
        halves = []
        for k in range(2):
            value = two_in[phase, k]
            for at in range(1, clusters):
                value = value + two_in[phase, 2 * at + k]
            halves.append(value)
        return jnp.concatenate(halves, axis=1)

    def correction_operand(amounts):
        a_h, a_l = split(jnp.concatenate([amounts, jnp.zeros((8, r), f32)], axis=0))
        return jnp.concatenate([a_h, a_l, a_h], axis=0)

    def load_operator(load, source, high, low):
        load.wait()
        step = 64

        def body(at, carry):
            rows = pl.ds(pl.multiple_of(at * step, step), step)
            high[rows, :], low[rows, :] = split(source[rows, :])
            return carry

        lax.fori_loop(0, m // step, body, 0)

    def edge_operator(high, low, rx_h, rx_l, k_h, k_l):
        wide_rx = jnp.concatenate([rx_h, rx_l], axis=0)
        for at in range(0, m, chunk):
            b_h, b_l = high[:, at:at + chunk], low[:, at:at + chunk]
            k_h[0:2 * p, at:at + chunk] = dot(pick[...], b_h).astype(bf16)
            k_l[0:2 * p, at:at + chunk] = dot(pick[...], b_l).astype(bf16)
            by_high = dot(wide_rx, b_h)
            rows = by_high[:32] + by_high[32:] + dot(rx_h, b_l)
            k_h[2 * p:, at:at + chunk], k_l[2 * p:, at:at + chunk] = split(rows)

    def apply(high, low, target):
        for at in range(0, m, chunk):
            target[at:at + chunk, :] = dot3(
                high[at:at + chunk, :], low[at:at + chunk, :], x_h[...], x_l[...])

    def spread(rows, e_h, e_l):
        return dot(place[rows, :], e_h) + dot(place[rows, :], e_l)

    def pieces():
        return [slice(at, at + chunk) for at in range(0, m, chunk)]

    def column_sum(x):
        return jnp.sum(x, axis=0, keepdims=True)

    loads[0].wait()
    gap_h, gap_l = split(gap[...])
    send_edges(0, dot(pick[...], gap_h) + dot(pick[...], gap_l))
    for side in range(2):
        @pl.when(has[side])
        def _():
            remote(rig_out.at[side], rig_in.at[side], rig_ss.at[side], rig_rs.at[side],
                   ids[side]).wait_recv()
    for side in range(2):
        n_h, n_l = split(rig_in[side])
        both = jnp.concatenate([n_h, n_l], axis=0)
        hot = pick[side * p:(side + 1) * p, :]
        spreaded = dot(both, hot)
        rx[2 * side * GROUP:(2 * side + 1) * GROUP, :] = spreaded[:GROUP] + spreaded[GROUP:]
    rx_h, rx_l = split(rx[...])
    send_sums(0, dot3(rx_h, rx_l, gap_h, gap_l)[:BLOCK], [])

    wait_recv(coarse_all.at[pl.ds(0, subs - 1)], co_rs.at[0])
    mine = coarse_all.at[pl.ds(c * subs, subs)]
    for i in range(1, clusters):
        remote(mine, mine, co_ss.at[1], co_rs.at[1], (cluster_peer(i), s)).start()

    rx_t = jnp.transpose(rx[...])
    t_h, t_l = split(rx_t)
    rxt3[...] = jnp.concatenate([t_h, t_h, t_l], axis=1)
    load_operator(loads[1], pre_in, pre_h, pre_l)

    wait_recv(coarse_all.at[pl.ds(0, (clusters - 1) * subs)], co_rs.at[1])
    for to_c in range(clusters):
        for k in range(2):
            for a in range(3):
                t = to_c * subs + base + k + a - 1
                valid = jnp.logical_and(t >= 0, t < total)
                rows = coarse_all[jnp.clip(t, 0, total - 1)]
                at = ((to_c * 2 + k) * 3 + a) * GROUP
                coarse_pick[at:at + GROUP, :] = jnp.where(valid, rows, 0.0)
    columns = subs * BLOCK
    i = lax.broadcasted_iota(jnp.int32, (wide, columns), 0)
    j = lax.broadcasted_iota(jnp.int32, (wide, columns), 1)
    j_mode = lax.rem(j, GROUP)
    source = (c * subs + lax.div(j, BLOCK) + lax.div(lax.rem(j, BLOCK), GROUP) - 1) * modes + j_mode
    hot = jnp.where(
        jnp.logical_and(jnp.logical_and(i == source, j_mode < modes), i < coarse), 1.0, 0.0
    ).astype(bf16)
    c_h, c_l = split(coarse_pick[...])
    shape = (clusters * 2 * BLOCK, columns)
    row = lax.rem(lax.broadcasted_iota(jnp.int32, shape, 0), BLOCK)
    col = lax.rem(lax.broadcasted_iota(jnp.int32, shape, 1), BLOCK)
    ones = jnp.where(jnp.logical_and(row == col, lax.rem(row, GROUP) >= modes), 1.0, 0.0)
    mix_h[...] = (dot(c_h, hot) + ones).astype(bf16)
    mix_l[...] = dot(c_l, hot).astype(bf16)

    pass_sums(0)
    rw_h, rw_l = split(rx[...] * row_weight)
    edge_operator(pre_h, pre_l, rw_h, rw_l, kp_h, kp_l)
    e_h, e_l = take_edges(0)
    operand = correction_operand(take_sums(0))
    norm0 = jnp.zeros((1, r), f32)
    for rows in pieces():
        w = weight[rows, :]
        res = gap[rows, :] + spread(rows, e_h, e_l)
        proj = res - dot(rxt3[rows, :], operand)
        r0[rows, :] = res
        p0[rows, :] = proj
        x_h[rows, :], x_l[rows, :] = split(w * proj)
        norm0 = norm0 + column_sum(w * res * res)

    def front(phase, k_h, k_l, sums):
        out = dot3(k_h[...], k_l[...], x_h[...], x_l[...])
        send_sums(phase, out[2 * p:2 * p + BLOCK], sums)
        send_edges(phase, out)

    front(1, kp_h, kp_l, [(6, norm0)])
    apply(pre_h, pre_l, u0)
    pass_sums(1)
    load_operator(loads[2], dual_in, dual_h, dual_l)
    edge_operator(dual_h, dual_l, rx_h, rx_l, kd_h, kd_l)
    pn0 = jnp.zeros((1, r), f32)
    for rows in pieces():
        pn0 = pn0 + column_sum(weight[rows, :] * p0[rows, :] * u0[rows, :])
    e_h, e_l = take_edges(1)
    sums = take_sums(1)
    norms_ref[0:1, :] = sums[6:7]
    operand = correction_operand(sums)
    for rows in pieces():
        smooth = weight[rows, :] * (u0[rows, :] + spread(rows, e_h, e_l))
        value = smooth - dot(rxt3[rows, :], operand)
        y0[rows, :] = value
        x_h[rows, :], x_l[rows, :] = split(value)

    front(2, kd_h, kd_l, [(6, pn0)])
    apply(dual_h, dual_l, q0)
    pass_sums(2)
    bend0 = jnp.zeros((1, r), f32)
    for rows in pieces():
        bend0 = bend0 + column_sum(y0[rows, :] * q0[rows, :])
    e_h, e_l = take_edges(2)
    sums = take_sums(2)
    pn0_sum = sums[6:7]
    operand = correction_operand(sums)
    for rows in pieces():
        image = q0[rows, :] + spread(rows, e_h, e_l)
        proj = image - dot(rxt3[rows, :], operand)
        im0[rows, :] = image
        g0[rows, :] = proj
        x_h[rows, :], x_l[rows, :] = split(weight[rows, :] * proj)

    front(3, kp_h, kp_l, [(6, bend0)])
    apply(pre_h, pre_l, tq)
    pass_sums(3)
    e_h, e_l = take_edges(3)
    sums = take_sums(3)
    step0 = pn0_sum / sums[6:7]
    bend0_sum = sums[6:7]
    operand = correction_operand(sums)
    pn1 = jnp.zeros((1, r), f32)
    norm1 = jnp.zeros((1, r), f32)
    for rows in pieces():
        w = weight[rows, :]
        smooth = w * (tq[rows, :] + spread(rows, e_h, e_l)) - dot(rxt3[rows, :], operand)
        value = y0[rows, :] - step0 * smooth
        y1[rows, :] = value
        x_h[rows, :], x_l[rows, :] = split(value)

    edges = dot3(kd_h[0:2 * p, :], kd_l[0:2 * p, :], x_h[...], x_l[...])
    send_edges(4, edges)
    for rows in pieces():
        w = weight[rows, :]
        res = r0[rows, :] - step0 * im0[rows, :]
        r0[rows, :] = res
        norm1 = norm1 + column_sum(w * res * res)
        pn1 = pn1 + column_sum(
            w * (p0[rows, :] - step0 * g0[rows, :]) * (u0[rows, :] - step0 * tq[rows, :]))
    apply(dual_h, dual_l, tq)
    own = jnp.zeros((1, r), f32)
    cross = jnp.zeros((1, r), f32)
    for rows in pieces():
        own = own + column_sum(y1[rows, :] * tq[rows, :])
        cross = cross + column_sum(y0[rows, :] * tq[rows, :] + y1[rows, :] * q0[rows, :])
    send_sums(4, jnp.zeros((BLOCK, r), f32), [(6, pn1), (7, norm1), (14, own), (15, cross)])
    e_h, e_l = take_edges(4)
    for rows in pieces():
        tq[rows, :] = tq[rows, :] + spread(rows, e_h, e_l)
    pass_sums(4)
    sums = take_sums(4)
    pn1_sum = sums[6:7]
    norms_ref[1:2, :] = sums[7:8]
    beta = pn1_sum / pn0_sum
    step1 = pn1_sum / (sums[14:15] + beta * sums[15:16] + beta * beta * bend0_sum)
    on_first = step0 + step1 * beta
    for rows in pieces():
        mult_ref[rows, :] = on_first * y0[rows, :] + step1 * y1[rows, :]
        res_ref[rows, :] = r0[rows, :] - step1 * (tq[rows, :] + beta * im0[rows, :])

    for side in range(2):
        @pl.when(has[side])
        def _():
            rig_copy(side).wait_send()
            for phase in range(PHASES):
                ex_copy(phase, side).wait_send()
    wait_send(coarse_all.at[pl.ds(0, subs - 1)], co_ss.at[0])
    wait_send(coarse_all.at[pl.ds(0, (clusters - 1) * subs)], co_ss.at[1])
    for phase in range(PHASES):
        wait_send(one_in.at[phase, pl.ds(0, subs - 1)], one_ss.at[phase])
        wait_send(two_in.at[phase, pl.ds(0, 2 * clusters - 1)], two_ss.at[phase])


def solution(mesh):
    clusters, subs = mesh.shape["cluster"], mesh.shape["sub"]

    def shards(dual_ops, boundary_solve_blocks, rigid_images, coarse_rows, gap_raw, row_maps):
        m, r = gap_raw.shape
        p = row_maps.shape[2]
        wide = -(-coarse_rows.shape[1] // 128) * 128
        total = clusters * subs
        field = pltpu.VMEM((m, r), f32)
        block16 = pltpu.VMEM((m, m), bf16)
        edge16 = pltpu.VMEM((2 * p + 32, m), bf16)
        mix16 = pltpu.VMEM((clusters * 2 * BLOCK, subs * BLOCK), bf16)
        sems = pltpu.SemaphoreType.DMA
        any_spec = pl.BlockSpec(memory_space=pl.ANY)
        vmem_spec = pl.BlockSpec(memory_space=pltpu.VMEM)
        return pl.pallas_call(
            functools.partial(kernel, clusters, subs),
            out_shape=(
                jax.ShapeDtypeStruct((m, r), f32),
                jax.ShapeDtypeStruct((m, r), f32),
                jax.ShapeDtypeStruct((2, r), f32),
            ),
            in_specs=[any_spec, any_spec, vmem_spec, vmem_spec, any_spec, vmem_spec],
            out_specs=(vmem_spec, vmem_spec, vmem_spec),
            scratch_shapes=[
                pltpu.VMEM((m, m), f32), pltpu.VMEM((m, m), f32),
                block16, block16, block16, block16, edge16, edge16, edge16, edge16,
                field, pltpu.VMEM((m, 2 * p), bf16), pltpu.VMEM((2 * p, m), bf16), field,
                pltpu.VMEM((32, m), f32), pltpu.VMEM((m, 96), bf16),
                pltpu.VMEM((m, r), bf16), pltpu.VMEM((m, r), bf16),
                field,
                pltpu.VMEM((total, GROUP, wide), f32),
                pltpu.VMEM((clusters * 2 * BLOCK, wide), f32),
                mix16, mix16,
                pltpu.VMEM((2, GROUP, p), f32), pltpu.VMEM((2, GROUP, p), f32),
                pltpu.VMEM((PHASES, 2, BLOCK, HALF), f32),
                pltpu.VMEM((PHASES, subs, BLOCK, HALF), f32),
                pltpu.VMEM((PHASES, 2 * clusters, BLOCK, HALF), f32),
                pltpu.VMEM((PHASES, 2 * clusters, BLOCK, HALF), f32),
                pltpu.VMEM((PHASES, 2, p, r), f32),
                pltpu.VMEM((PHASES, 2, p, r), f32),
                sems((3,)), sems((2,)), sems((2,)), sems((2,)), sems((2,)),
                sems((PHASES,)), sems((PHASES,)), sems((PHASES,)), sems((PHASES,)),
                sems((PHASES, 2)), sems((PHASES, 2)),
            ],
            compiler_params=pltpu.CompilerParams(
                collective_id=0, has_side_effects=True, vmem_limit_bytes=58 * 1024 * 1024),
        )(dual_ops, boundary_solve_blocks, rigid_images, coarse_rows, gap_raw, row_maps)

    rows = P(("cluster", "sub"), None)
    return jax.shard_map(
        shards,
        mesh=mesh,
        in_specs=(rows, rows, rows, rows, rows, P(("cluster", "sub"), None, None)),
        out_specs=(rows, rows, P()),
        check_vma=False,
    )
```

time: 442 us -> 70.4 us (0.16); the launches traced: 435 us -> 70.1 us
  blocking collectives: 255 us -> 0 us
  Pallas kernels: 0 us -> 64.4 us
  other arithmetic: 50.1 us -> 0 us
  matrix products: 46.7 us -> 0 us
  local copies, waits for them, and re-layouts: 40.4 us -> 5.11 us
  starting transfers between devices: 33.5 us -> 0 us
  waiting for transfers between devices: 6.97 us -> 0 us
    psum x3 -> x0, blocking collectives: 136 us -> none  [the longest x2 91 us: project(): total = lax.psum(partial_value, ('cluster', 'sub'))]
    all_gather x8 -> x0, blocking collectives: 120 us -> none  [the longest x4 79.7 us: project(): nearby = lax.all_gather(kernel_basis_matrix, 'sub', axis=0, tiled=True)]
    pallas_call x0 -> x1, Pallas kernels: none -> 64.4 us  [shards(): pl.pallas_call(functools.partial(kernel, clusters, subs), out_shape=(jax....]
    dot_general x16 -> x0, matrix products: 46.7 us -> none  [the longest x2 19.7 us: shards(): jnp.dot(boundary_solve_blocks, interface_weights * projected_residual, pr...]
    scatter-add x18 -> x0, other arithmetic: 37.6 us -> none  [the longest x10 20.1 us: assemble_dual(): return deformation_vector.at[left_neighbour_rows].add(from_left).at[right...]
    ppermute x18 -> x0, starting transfers between devices: 33.5 us -> none  [passed_along(): lax.ppermute(value, axis, [(source, source + steps) for source in range(i...]
    gather x18 -> x0, local copies, waits for them, and re-layouts: 24.3 us -> none  [the longest x5 6.93 us: assemble_dual(): outgoing_left = deformation_vector[left_neighbour_rows]]
    dot_general x8 -> x0, local copies, waits for them, and re-layouts: 9.49 us -> none  [the longest x4 4.75 us: project(): jnp.einsum('km,kr->mr', rigid_images, load_amounts, precision=finest_tier)]
  transfers between devices with their start and end apart: 18 -> 0, of which waited for: 5 -> 0; matrix products, arithmetic and copies ran while one was open for 8% -> 0% of each run, Pallas kernels for 0% -> 0%
where the time goes in v1:
time: 70.4 us; the launch traced here: 70.1 us
  Pallas kernels  64.4 us (91%)
  local copies, waits for them, and re-layouts  5.11 us (7%)
    pallas_call x1, Pallas kernels, shards(): pl.pallas_call(functools.partial(kernel, clusters, subs), out_shape=(jax....  64.4 us
    unnamed x5, local copies, waits for them, and re-layouts  5.11 us

profile of v1, /device:TPU:0, one launch (start us, length us, event | category | flops | bytes accessed | tf_op | source)
XLA Modules:
  0.0 70.1 jit_solution(7073453769220338627)
XLA Ops:
  0.6 64.4 %shard_map.85 = (f32[1024,256]{1,0:T(8,128)}, f32[1024,256]{1,0:T(8,128)}, f32[2,256]{1,0:T(2,128)}) custom-call(f32[1024,1024]{1,0:T(8,128)} %dual_hbm.1, f32[1024,1024]{1,0:T(8,128)} %pre_hbm.1, f32[6,1024]{1,0:T(8,128)} %rigid_ref.1, f32[6,192]{1,0:T(8,128)} %coarse_ref.1, f32[1024,256]{1,0:T(8,128)} %gap_hbm.1, s32[1,2,128]{2,1,0:T(2,128)} %maps_ref.1), custom_call_target="tpu_custom_call" | custom-call | tf_op jit(solution)/shard_map/pallas_call | solution.py:441
  65.0 0.0 copy-start
  65.0 2.3 %copy.12 = f32[1024,256]{1,0:T(8,128)} copy(f32[1024,256]{1,0:T(8,128)} %get-tuple-element.6) | data formatting | bytes 2097152
  67.3 2.3 %copy.13 = f32[1024,256]{1,0:T(8,128)} copy(f32[1024,256]{1,0:T(8,128)} %get-tuple-element.7) | data formatting | bytes 2097152
  69.5 0.0 copy-done
  69.6 0.6 copy.14
Async XLA Ops:
  65.0 4.5 %copy-start = (f32[2,256]{1,0:T(2,128)S(1)}, f32[2,256]{1,0:T(2,128)}, u32[]{:S(2)}) copy-start(f32[2,256]{1,0:T(2,128)} %get-tuple-element.8) | copy-start | bytes 6148

commit v2 on v1

--- a/solution.py
+++ b/solution.py
@@ -39,7 +39,7 @@
 def kernel(clusters, subs, dual_hbm, pre_hbm, rigid_ref, coarse_ref, gap_hbm, maps_ref,
            mult_ref, res_ref, norms_ref,
            dual_in, pre_in, dual_h, dual_l, pre_h, pre_l, kd_h, kd_l, kp_h, kp_l,
-           gap, place, pick, weight, rx, rxt3, x_h, x_l,
+           gap, place, pick, weight, rx, rxt3, rxw3, fx3, kpc3, kdc3, out_k, keep, x_h, x_l,
            q0,
            coarse_all, coarse_pick, mix_h, mix_l, rig_out, rig_in,
            one_out, one_in, two_out, two_in, ex_out, ex_in,
@@ -106,8 +106,12 @@
         hot = jnp.where(
             lax.broadcasted_iota(jnp.int32, (chunk, 2 * p), 0) + at == row_list, 1.0, 0.0)
         place[at:at + chunk, :] = hot.astype(bf16)
-        column = 1.0 - jnp.sum(hot * side_half, axis=1, keepdims=True)
-        weight[at:at + chunk, :] = jnp.broadcast_to(column, (chunk, r))
+
+    def set_weight():
+        for at in range(0, m, chunk):
+            hot = place[at:at + chunk, :].astype(f32)
+            column = 1.0 - jnp.sum(hot * side_half, axis=1, keepdims=True)
+            weight[at:at + chunk, :] = jnp.broadcast_to(column, (chunk, r))
 
     rx[...] = jnp.zeros_like(rx)
     rx[GROUP:GROUP + modes, :] = rigid_ref[...]
@@ -232,20 +236,23 @@
 
         lax.fori_loop(0, m // step, body, 0)
 
-    def edge_operator(high, low, rx_h, rx_l, k_h, k_l):
-        wide_rx = jnp.concatenate([rx_h, rx_l], axis=0)
+    def edge_operator(high, low, k_rx, k_h, k_l, kc3):
+        wide_rx = jnp.concatenate(k_rx, axis=0)
         for at in range(0, m, chunk):
             b_h, b_l = high[:, at:at + chunk], low[:, at:at + chunk]
             k_h[0:2 * p, at:at + chunk] = dot(pick[...], b_h).astype(bf16)
             k_l[0:2 * p, at:at + chunk] = dot(pick[...], b_l).astype(bf16)
             by_high = dot(wide_rx, b_h)
-            rows = by_high[:32] + by_high[32:] + dot(rx_h, b_l)
+            rows = by_high[:32] + by_high[32:] + dot(k_rx[0], b_l)
             k_h[2 * p:, at:at + chunk], k_l[2 * p:, at:at + chunk] = split(rows)
+        weighted = kc3 is kpc3
+        t_h = rxw3[:, 0:32] if weighted else rxt3[:, 0:32]
+        t_l = rxw3[:, 64:96] if weighted else rxt3[:, 64:96]
+        c_h, c_l = split(dot3(k_h[...], k_l[...], t_h, t_l))
+        kc3[...] = jnp.concatenate([c_h, c_h, c_l], axis=1)
 
     def apply(high, low, target):
-        for at in range(0, m, chunk):
-            target[at:at + chunk, :] = dot3(
-                high[at:at + chunk, :], low[at:at + chunk, :], x_h[...], x_l[...])
+        target[...] = dot(high[...], x_h[...]) + dot(high[...], x_l[...]) + dot(low[...], x_h[...])
 
     def spread(rows, e_h, e_l):
         return dot(place[rows, :], e_h) + dot(place[rows, :], e_l)
@@ -255,10 +262,21 @@
 
     def column_sum(x):
         return jnp.sum(x, axis=0, keepdims=True)
+
+    def front(k_h, k_l):
+        out_k[...] = dot3(k_h[...], k_l[...], x_h[...], x_l[...])
+
+    def send_front(phase, kc3, operand, sums):
+        out = out_k[...] - dot(kc3[...], operand)
+        send_sums(phase, out[2 * p:2 * p + BLOCK], sums)
+        send_edges(phase, out)
+        return out
 
     loads[0].wait()
     gap_h, gap_l = split(gap[...])
     send_edges(0, dot(pick[...], gap_h) + dot(pick[...], gap_l))
+    set_weight()
+    load_operator(loads[1], pre_in, pre_h, pre_l)
     for side in range(2):
         @pl.when(has[side])
         def _():
@@ -278,11 +296,24 @@
     for i in range(1, clusters):
         remote(mine, mine, co_ss.at[1], co_rs.at[1], (cluster_peer(i), s)).start()
 
-    rx_t = jnp.transpose(rx[...])
-    t_h, t_l = split(rx_t)
-    rxt3[...] = jnp.concatenate([t_h, t_h, t_l], axis=1)
-    load_operator(loads[1], pre_in, pre_h, pre_l)
-
+    rw = rx[...] * row_weight
+    for source, target in ((rx[...], rxt3), (rw, rxw3)):
+        t_h, t_l = split(jnp.transpose(source))
+        target[...] = jnp.concatenate([t_h, t_h, t_l], axis=1)
+    rw_h, rw_l = split(rw)
+
+    columns = subs * BLOCK
+    i = lax.broadcasted_iota(jnp.int32, (wide, columns), 0)
+    j = lax.broadcasted_iota(jnp.int32, (wide, columns), 1)
+    j_mode = lax.rem(j, GROUP)
+    source = (c * subs + lax.div(j, BLOCK) + lax.div(lax.rem(j, BLOCK), GROUP) - 1) * modes + j_mode
+    hot = jnp.where(
+        jnp.logical_and(jnp.logical_and(i == source, j_mode < modes), i < coarse), 1.0, 0.0
+    ).astype(bf16)
+    shape = (clusters * 2 * BLOCK, columns)
+    row = lax.rem(lax.broadcasted_iota(jnp.int32, shape, 0), BLOCK)
+    col = lax.rem(lax.broadcasted_iota(jnp.int32, shape, 1), BLOCK)
+    ones = jnp.where(jnp.logical_and(row == col, lax.rem(row, GROUP) >= modes), 1.0, 0.0)
     wait_recv(coarse_all.at[pl.ds(0, (clusters - 1) * subs)], co_rs.at[1])
     for to_c in range(clusters):
         for k in range(2):
@@ -292,109 +323,105 @@
                 rows = coarse_all[jnp.clip(t, 0, total - 1)]
                 at = ((to_c * 2 + k) * 3 + a) * GROUP
                 coarse_pick[at:at + GROUP, :] = jnp.where(valid, rows, 0.0)
-    columns = subs * BLOCK
-    i = lax.broadcasted_iota(jnp.int32, (wide, columns), 0)
-    j = lax.broadcasted_iota(jnp.int32, (wide, columns), 1)
-    j_mode = lax.rem(j, GROUP)
-    source = (c * subs + lax.div(j, BLOCK) + lax.div(lax.rem(j, BLOCK), GROUP) - 1) * modes + j_mode
-    hot = jnp.where(
-        jnp.logical_and(jnp.logical_and(i == source, j_mode < modes), i < coarse), 1.0, 0.0
-    ).astype(bf16)
     c_h, c_l = split(coarse_pick[...])
-    shape = (clusters * 2 * BLOCK, columns)
-    row = lax.rem(lax.broadcasted_iota(jnp.int32, shape, 0), BLOCK)
-    col = lax.rem(lax.broadcasted_iota(jnp.int32, shape, 1), BLOCK)
-    ones = jnp.where(jnp.logical_and(row == col, lax.rem(row, GROUP) >= modes), 1.0, 0.0)
     mix_h[...] = (dot(c_h, hot) + ones).astype(bf16)
     mix_l[...] = dot(c_l, hot).astype(bf16)
 
     pass_sums(0)
-    rw_h, rw_l = split(rx[...] * row_weight)
-    edge_operator(pre_h, pre_l, rw_h, rw_l, kp_h, kp_l)
+    edge_operator(pre_h, pre_l, (rw_h, rw_l), kp_h, kp_l, kpc3)
     e_h, e_l = take_edges(0)
-    operand = correction_operand(take_sums(0))
     norm0 = jnp.zeros((1, r), f32)
     for rows in pieces():
         w = weight[rows, :]
         res = gap[rows, :] + spread(rows, e_h, e_l)
-        proj = res - dot(rxt3[rows, :], operand)
         r0[rows, :] = res
+        x_h[rows, :], x_l[rows, :] = split(w * res)
+        norm0 = norm0 + column_sum(w * res * res)
+    front(kp_h, kp_l)
+    operand = correction_operand(take_sums(0))
+
+    send_front(1, kpc3, operand, [(6, norm0)])
+    for rows in pieces():
+        proj = r0[rows, :] - dot(rxt3[rows, :], operand)
         p0[rows, :] = proj
-        x_h[rows, :], x_l[rows, :] = split(w * proj)
-        norm0 = norm0 + column_sum(w * res * res)
-
-    def front(phase, k_h, k_l, sums):
-        out = dot3(k_h[...], k_l[...], x_h[...], x_l[...])
-        send_sums(phase, out[2 * p:2 * p + BLOCK], sums)
-        send_edges(phase, out)
-
-    front(1, kp_h, kp_l, [(6, norm0)])
+        x_h[rows, :], x_l[rows, :] = split(weight[rows, :] * proj)
     apply(pre_h, pre_l, u0)
     pass_sums(1)
     load_operator(loads[2], dual_in, dual_h, dual_l)
-    edge_operator(dual_h, dual_l, rx_h, rx_l, kd_h, kd_l)
+    edge_operator(dual_h, dual_l, (rx_h, rx_l), kd_h, kd_l, kdc3)
+    for at in range(0, m, chunk):
+        rows = slice(at, at + chunk)
+        t_h, t_l = split(dot3(dual_h[rows, :], dual_l[rows, :], rxt3[:, 0:32], rxt3[:, 64:96]))
+        fx3[rows, :] = jnp.concatenate([t_h, t_h, t_l], axis=1)
+    e_h, e_l = take_edges(1)
     pn0 = jnp.zeros((1, r), f32)
     for rows in pieces():
-        pn0 = pn0 + column_sum(weight[rows, :] * p0[rows, :] * u0[rows, :])
-    e_h, e_l = take_edges(1)
+        w, u = weight[rows, :], u0[rows, :]
+        pn0 = pn0 + column_sum(w * p0[rows, :] * u)
+        smooth = w * (u + spread(rows, e_h, e_l))
+        y0[rows, :] = smooth
+        x_h[rows, :], x_l[rows, :] = split(smooth)
+    front(kd_h, kd_l)
     sums = take_sums(1)
+    operand = correction_operand(sums)
+
+    edges0 = send_front(2, kdc3, operand, [(6, pn0)])[:2 * p]
+    keep[...] = edges0
     norms_ref[0:1, :] = sums[6:7]
-    operand = correction_operand(sums)
-    for rows in pieces():
-        smooth = weight[rows, :] * (u0[rows, :] + spread(rows, e_h, e_l))
-        value = smooth - dot(rxt3[rows, :], operand)
+    for rows in pieces():
+        value = y0[rows, :] - dot(rxt3[rows, :], operand)
         y0[rows, :] = value
         x_h[rows, :], x_l[rows, :] = split(value)
-
-    front(2, kd_h, kd_l, [(6, pn0)])
     apply(dual_h, dual_l, q0)
     pass_sums(2)
+    e_h, e_l = take_edges(2)
     bend0 = jnp.zeros((1, r), f32)
     for rows in pieces():
-        bend0 = bend0 + column_sum(y0[rows, :] * q0[rows, :])
-    e_h, e_l = take_edges(2)
+        q = q0[rows, :]
+        bend0 = bend0 + column_sum(y0[rows, :] * q)
+        image = q + spread(rows, e_h, e_l)
+        im0[rows, :] = image
+        x_h[rows, :], x_l[rows, :] = split(weight[rows, :] * image)
+    front(kp_h, kp_l)
     sums = take_sums(2)
     pn0_sum = sums[6:7]
     operand = correction_operand(sums)
-    for rows in pieces():
-        image = q0[rows, :] + spread(rows, e_h, e_l)
-        proj = image - dot(rxt3[rows, :], operand)
-        im0[rows, :] = image
+
+    send_front(3, kpc3, operand, [(6, bend0)])
+    for rows in pieces():
+        proj = im0[rows, :] - dot(rxt3[rows, :], operand)
         g0[rows, :] = proj
         x_h[rows, :], x_l[rows, :] = split(weight[rows, :] * proj)
-
-    front(3, kp_h, kp_l, [(6, bend0)])
     apply(pre_h, pre_l, tq)
     pass_sums(3)
     e_h, e_l = take_edges(3)
+    for rows in pieces():
+        smooth = weight[rows, :] * (tq[rows, :] + spread(rows, e_h, e_l))
+        y1[rows, :] = smooth
+        x_h[rows, :], x_l[rows, :] = split(smooth)
+    front(kd_h, kd_l)
+    apply(dual_h, dual_l, gap)
     sums = take_sums(3)
-    step0 = pn0_sum / sums[6:7]
     bend0_sum = sums[6:7]
+    step0 = pn0_sum / bend0_sum
     operand = correction_operand(sums)
-    pn1 = jnp.zeros((1, r), f32)
-    norm1 = jnp.zeros((1, r), f32)
-    for rows in pieces():
-        w = weight[rows, :]
-        smooth = w * (tq[rows, :] + spread(rows, e_h, e_l)) - dot(rxt3[rows, :], operand)
-        value = y0[rows, :] - step0 * smooth
-        y1[rows, :] = value
-        x_h[rows, :], x_l[rows, :] = split(value)
-
-    edges = dot3(kd_h[0:2 * p, :], kd_l[0:2 * p, :], x_h[...], x_l[...])
-    send_edges(4, edges)
-    for rows in pieces():
-        w = weight[rows, :]
-        res = r0[rows, :] - step0 * im0[rows, :]
+
+    send_edges(4, keep[...] - step0 * (out_k[0:2 * p] - dot(kdc3[0:2 * p], operand)))
+    zero = jnp.zeros((1, r), f32)
+    pn1, norm1, own, cross = zero, zero, zero, zero
+    for rows in pieces():
+        w, old_y, old_q, image = weight[rows, :], y0[rows, :], q0[rows, :], im0[rows, :]
+        res = r0[rows, :] - step0 * image
         r0[rows, :] = res
         norm1 = norm1 + column_sum(w * res * res)
         pn1 = pn1 + column_sum(
             w * (p0[rows, :] - step0 * g0[rows, :]) * (u0[rows, :] - step0 * tq[rows, :]))
-    apply(dual_h, dual_l, tq)
-    own = jnp.zeros((1, r), f32)
-    cross = jnp.zeros((1, r), f32)
-    for rows in pieces():
-        own = own + column_sum(y1[rows, :] * tq[rows, :])
-        cross = cross + column_sum(y0[rows, :] * tq[rows, :] + y1[rows, :] * q0[rows, :])
+        value = old_y - step0 * (y1[rows, :] - dot(rxt3[rows, :], operand))
+        y1[rows, :] = value
+        q = old_q - step0 * (gap[rows, :] - dot(fx3[rows, :], operand))
+        tq[rows, :] = q
+        own = own + column_sum(value * q)
+        cross = cross + column_sum(old_y * q + value * old_q)
     send_sums(4, jnp.zeros((BLOCK, r), f32), [(6, pn1), (7, norm1), (14, own), (15, cross)])
     e_h, e_l = take_edges(4)
     for rows in pieces():
@@ -421,6 +448,15 @@
     for phase in range(PHASES):
         wait_send(one_in.at[phase, pl.ds(0, subs - 1)], one_ss.at[phase])
         wait_send(two_in.at[phase, pl.ds(0, 2 * clusters - 1)], two_ss.at[phase])
+
+
+def write_out(a, b, c, a_out, b_out, c_out, sem):
+    copies = [pltpu.make_async_copy(src, dst, sem.at[at])
+              for at, (src, dst) in enumerate(((a, a_out), (b, b_out), (c, c_out)))]
+    for copy in copies:
+        copy.start()
+    for copy in copies:
+        copy.wait()
 
 
 def solution(mesh):
@@ -438,20 +474,19 @@
         sems = pltpu.SemaphoreType.DMA
         any_spec = pl.BlockSpec(memory_space=pl.ANY)
         vmem_spec = pl.BlockSpec(memory_space=pltpu.VMEM)
-        return pl.pallas_call(
+        held = pl.pallas_call(
             functools.partial(kernel, clusters, subs),
-            out_shape=(
-                jax.ShapeDtypeStruct((m, r), f32),
-                jax.ShapeDtypeStruct((m, r), f32),
-                jax.ShapeDtypeStruct((2, r), f32),
-            ),
+            out_shape=(field, field, pltpu.VMEM((2, r), f32)),
             in_specs=[any_spec, any_spec, vmem_spec, vmem_spec, any_spec, vmem_spec],
             out_specs=(vmem_spec, vmem_spec, vmem_spec),
             scratch_shapes=[
                 pltpu.VMEM((m, m), f32), pltpu.VMEM((m, m), f32),
                 block16, block16, block16, block16, edge16, edge16, edge16, edge16,
                 field, pltpu.VMEM((m, 2 * p), bf16), pltpu.VMEM((2 * p, m), bf16), field,
-                pltpu.VMEM((32, m), f32), pltpu.VMEM((m, 96), bf16),
+                pltpu.VMEM((32, m), f32),
+                pltpu.VMEM((m, 96), bf16), pltpu.VMEM((m, 96), bf16), pltpu.VMEM((m, 96), bf16),
+                pltpu.VMEM((2 * p + 32, 96), bf16), pltpu.VMEM((2 * p + 32, 96), bf16),
+                pltpu.VMEM((2 * p + 32, r), f32), pltpu.VMEM((2 * p, r), f32),
                 pltpu.VMEM((m, r), bf16), pltpu.VMEM((m, r), bf16),
                 field,
                 pltpu.VMEM((total, GROUP, wide), f32),
@@ -471,6 +506,13 @@
             compiler_params=pltpu.CompilerParams(
                 collective_id=0, has_side_effects=True, vmem_limit_bytes=58 * 1024 * 1024),
         )(dual_ops, boundary_solve_blocks, rigid_images, coarse_rows, gap_raw, row_maps)
+        return pl.pallas_call(
+            write_out,
+            out_shape=tuple(jax.ShapeDtypeStruct(h.shape, h.dtype) for h in held),
+            in_specs=[vmem_spec] * 3,
+            out_specs=(any_spec,) * 3,
+            scratch_shapes=[sems((3,))],
+        )(*held)
 
     rows = P(("cluster", "sub"), None)
     return jax.shard_map(

time: 70.4 us -> 73.1 us (1.038)
  Pallas kernels: 64.4 us -> 69.5 us
  local copies, waits for them, and re-layouts: 5.11 us -> 2.55 us
    pallas_call x1 -> x2, Pallas kernels: 64.4 us -> 69.5 us  [the longest x1 66.6 us: shards(): pl.pallas_call(functools.partial(kernel, clusters, subs), out_shape=(fiel...]
    unnamed x5 -> x6, local copies, waits for them, and re-layouts: 5.11 us -> 2.55 us
where the time goes in v2:
time: 73.1 us; the launch traced here: 72.9 us
  Pallas kernels  69.5 us (95%)
  local copies, waits for them, and re-layouts  2.55 us (3%)
  between operations  0.83 us (1%)
    pallas_call x1, Pallas kernels, shards(): pl.pallas_call(functools.partial(kernel, clusters, subs), out_shape=(fiel...  66.6 us
    pallas_call x1, Pallas kernels, shards(): pl.pallas_call(write_out, out_shape=tuple((jax.ShapeDtypeStruct(h.shape,...  2.88 us
    unnamed x6, local copies, waits for them, and re-layouts  2.55 us

profile of v2, /device:TPU:0, one launch (start us, length us, event | category | flops | bytes accessed | tf_op | source)
XLA Modules:
  0.0 72.9 jit_solution(8433129914293301880)
XLA Ops:
  0.6 66.6 %shard_map.85 = (f32[1024,256]{1,0:T(8,128)S(1)}, f32[1024,256]{1,0:T(8,128)S(1)}, f32[2,256]{1,0:T(2,128)S(1)}) custom-call(f32[1024,1024]{1,0:T(8,128)} %dual_hbm.1, f32[1024,1024]{1,0:T(8,128)} %pre_hbm.1, f32[6,1024]{1,0:T(8,128)} %rigid_ref.1, f32[6,192]{1,0:T(8,128)} %coarse_ref.1, f32[1024,256]{1,0:T(8,128)} %gap_hbm.1, s32[1,2,128]{2,1,0:T(2,128)} %maps_ref.1), custom_call_target="tpu_custom_call" | custom-call | tf_op jit(solution)/shard_map/pallas_call | solution.py:477
  67.3 0.0 copy-start
  67.3 1.0 %copy-done = f32[1024,256]{1,0:T(8,128)} copy-done((f32[1024,256]{1,0:T(8,128)}, f32[1024,256]{1,0:T(8,128)S(1)}, u32[]{:S(2)}) %copy-start) | copy-done | bytes 1048600
  68.2 0.0 copy-start.1
  68.2 1.0 %copy-done.1 = f32[1024,256]{1,0:T(8,128)} copy-done((f32[1024,256]{1,0:T(8,128)}, f32[1024,256]{1,0:T(8,128)S(1)}, u32[]{:S(2)}) %copy-start.1) | copy-done | bytes 1048600
  69.2 0.0 copy-start.2
  69.2 0.6 copy-done.2
  69.8 2.9 %shard_map.86 = (f32[1024,256]{1,0:T(8,128)}, f32[1024,256]{1,0:T(8,128)}, f32[2,256]{1,0:T(2,128)}) custom-call(f32[1024,256]{1,0:T(8,128)} %copy-done, f32[1024,256]{1,0:T(8,128)} %copy-done.1, f32[2,256]{1,0:T(2,128)} %copy-done.2), custom_call_target="tpu_custom_call" | custom-call | tf_op jit(solution)/shard_map/pallas_call | solution.py:509
Async XLA Ops:
  67.3 1.0 %copy-start = (f32[1024,256]{1,0:T(8,128)}, f32[1024,256]{1,0:T(8,128)S(1)}, u32[]{:S(2)}) copy-start(f32[1024,256]{1,0:T(8,128)S(1)} %get-tuple-element.6.a) | copy-start | bytes 3145732
  68.2 1.0 %copy-start.1 = (f32[1024,256]{1,0:T(8,128)}, f32[1024,256]{1,0:T(8,128)S(1)}, u32[]{:S(2)}) copy-start(f32[1024,256]{1,0:T(8,128)S(1)} %get-tuple-element.7.b) | copy-start | bytes 3145732
  69.2 0.6 copy-start.2

commit v3 on v2

--- a/solution.py
+++ b/solution.py
@@ -51,6 +51,7 @@
     r = gap.shape[1]
     wide = coarse_all.shape[2]
     chunk = m // 4
+    piece = m // 8
     c, s = lax.axis_index("cluster"), lax.axis_index("sub")
     me = c * subs + s
     core = lax.rem(s, 2)
@@ -102,16 +103,21 @@
     row_weight = (1.0 - left_half * jnp.sum(pick_f[:p], axis=0, keepdims=True)
                   - right_half * jnp.sum(pick_f[p:], axis=0, keepdims=True))
     side_half = jnp.where(lax.broadcasted_iota(jnp.int32, (1, 2 * p), 1) < p, left_half, right_half)
-    for at in range(0, m, chunk):
+
+    def set_place(at, carry):
+        rows = pl.ds(pl.multiple_of(at * piece, piece), piece)
         hot = jnp.where(
-            lax.broadcasted_iota(jnp.int32, (chunk, 2 * p), 0) + at == row_list, 1.0, 0.0)
-        place[at:at + chunk, :] = hot.astype(bf16)
-
-    def set_weight():
-        for at in range(0, m, chunk):
-            hot = place[at:at + chunk, :].astype(f32)
-            column = 1.0 - jnp.sum(hot * side_half, axis=1, keepdims=True)
-            weight[at:at + chunk, :] = jnp.broadcast_to(column, (chunk, r))
+            lax.broadcasted_iota(jnp.int32, (piece, 2 * p), 0) + at * piece == row_list, 1.0, 0.0)
+        place[rows, :] = hot.astype(bf16)
+        return carry
+
+    lax.fori_loop(0, m // piece, set_place, 0)
+
+    def set_weight(at, carry):
+        rows = pl.ds(pl.multiple_of(at * piece, piece), piece)
+        column = 1.0 - jnp.sum(place[rows, :].astype(f32) * side_half, axis=1, keepdims=True)
+        weight[rows, :] = jnp.broadcast_to(column, (piece, r))
+        return carry
 
     rx[...] = jnp.zeros_like(rx)
     rx[GROUP:GROUP + modes, :] = rigid_ref[...]
@@ -238,13 +244,18 @@
 
     def edge_operator(high, low, k_rx, k_h, k_l, kc3):
         wide_rx = jnp.concatenate(k_rx, axis=0)
-        for at in range(0, m, chunk):
-            b_h, b_l = high[:, at:at + chunk], low[:, at:at + chunk]
-            k_h[0:2 * p, at:at + chunk] = dot(pick[...], b_h).astype(bf16)
-            k_l[0:2 * p, at:at + chunk] = dot(pick[...], b_l).astype(bf16)
+
+        def body(at, carry):
+            cols = pl.ds(pl.multiple_of(at * chunk, chunk), chunk)
+            b_h, b_l = high[:, cols], low[:, cols]
+            k_h[0:2 * p, cols] = dot(pick[...], b_h).astype(bf16)
+            k_l[0:2 * p, cols] = dot(pick[...], b_l).astype(bf16)
             by_high = dot(wide_rx, b_h)
             rows = by_high[:32] + by_high[32:] + dot(k_rx[0], b_l)
-            k_h[2 * p:, at:at + chunk], k_l[2 * p:, at:at + chunk] = split(rows)
+            k_h[2 * p:, cols], k_l[2 * p:, cols] = split(rows)
+            return carry
+
+        lax.fori_loop(0, m // chunk, body, 0)
         weighted = kc3 is kpc3
         t_h = rxw3[:, 0:32] if weighted else rxt3[:, 0:32]
         t_l = rxw3[:, 64:96] if weighted else rxt3[:, 64:96]
@@ -252,13 +263,21 @@
         kc3[...] = jnp.concatenate([c_h, c_h, c_l], axis=1)
 
     def apply(high, low, target):
-        target[...] = dot(high[...], x_h[...]) + dot(high[...], x_l[...]) + dot(low[...], x_h[...])
+        def body(at, carry):
+            rows = pl.ds(pl.multiple_of(at * chunk, chunk), chunk)
+            target[rows, :] = dot3(high[rows, :], low[rows, :], x_h[...], x_l[...])
+            return carry
+
+        lax.fori_loop(0, m // chunk, body, 0)
 
     def spread(rows, e_h, e_l):
         return dot(place[rows, :], e_h) + dot(place[rows, :], e_l)
 
-    def pieces():
-        return [slice(at, at + chunk) for at in range(0, m, chunk)]
+    def sweep(body, start=0):
+        def step(at, carry):
+            return body(pl.ds(pl.multiple_of(at * piece, piece), piece), carry)
+
+        return lax.fori_loop(0, m // piece, step, start)
 
     def column_sum(x):
         return jnp.sum(x, axis=0, keepdims=True)
@@ -273,9 +292,14 @@
         return out
 
     loads[0].wait()
-    gap_h, gap_l = split(gap[...])
-    send_edges(0, dot(pick[...], gap_h) + dot(pick[...], gap_l))
-    set_weight()
+
+    def split_gap(rows, carry):
+        x_h[rows, :], x_l[rows, :] = split(gap[rows, :])
+        return carry
+
+    sweep(split_gap)
+    send_edges(0, dot(pick[...], x_h[...]) + dot(pick[...], x_l[...]))
+    lax.fori_loop(0, m // piece, set_weight, 0)
     load_operator(loads[1], pre_in, pre_h, pre_l)
     for side in range(2):
         @pl.when(has[side])
@@ -289,7 +313,7 @@
         spreaded = dot(both, hot)
         rx[2 * side * GROUP:(2 * side + 1) * GROUP, :] = spreaded[:GROUP] + spreaded[GROUP:]
     rx_h, rx_l = split(rx[...])
-    send_sums(0, dot3(rx_h, rx_l, gap_h, gap_l)[:BLOCK], [])
+    send_sums(0, dot3(rx_h, rx_l, x_h[...], x_l[...])[:BLOCK], [])
 
     wait_recv(coarse_all.at[pl.ds(0, subs - 1)], co_rs.at[0])
     mine = coarse_all.at[pl.ds(c * subs, subs)]
@@ -331,36 +355,50 @@
     edge_operator(pre_h, pre_l, (rw_h, rw_l), kp_h, kp_l, kpc3)
     e_h, e_l = take_edges(0)
     norm0 = jnp.zeros((1, r), f32)
-    for rows in pieces():
+    def sweep_1(rows, carry):
+        norm0, = carry
         w = weight[rows, :]
         res = gap[rows, :] + spread(rows, e_h, e_l)
         r0[rows, :] = res
         x_h[rows, :], x_l[rows, :] = split(w * res)
         norm0 = norm0 + column_sum(w * res * res)
+        return (norm0,)
+
+    norm0, = sweep(sweep_1, (norm0,))
     front(kp_h, kp_l)
     operand = correction_operand(take_sums(0))
 
     send_front(1, kpc3, operand, [(6, norm0)])
-    for rows in pieces():
+    def sweep_2(rows, carry):
         proj = r0[rows, :] - dot(rxt3[rows, :], operand)
         p0[rows, :] = proj
         x_h[rows, :], x_l[rows, :] = split(weight[rows, :] * proj)
+        return carry
+
+    sweep(sweep_2)
     apply(pre_h, pre_l, u0)
     pass_sums(1)
     load_operator(loads[2], dual_in, dual_h, dual_l)
     edge_operator(dual_h, dual_l, (rx_h, rx_l), kd_h, kd_l, kdc3)
-    for at in range(0, m, chunk):
-        rows = slice(at, at + chunk)
+
+    def set_fx(rows, carry):
         t_h, t_l = split(dot3(dual_h[rows, :], dual_l[rows, :], rxt3[:, 0:32], rxt3[:, 64:96]))
         fx3[rows, :] = jnp.concatenate([t_h, t_h, t_l], axis=1)
+        return carry
+
+    sweep(set_fx)
     e_h, e_l = take_edges(1)
     pn0 = jnp.zeros((1, r), f32)
-    for rows in pieces():
+    def sweep_3(rows, carry):
+        pn0, = carry
         w, u = weight[rows, :], u0[rows, :]
         pn0 = pn0 + column_sum(w * p0[rows, :] * u)
         smooth = w * (u + spread(rows, e_h, e_l))
         y0[rows, :] = smooth
         x_h[rows, :], x_l[rows, :] = split(smooth)
+        return (pn0,)
+
+    pn0, = sweep(sweep_3, (pn0,))
     front(kd_h, kd_l)
     sums = take_sums(1)
     operand = correction_operand(sums)
@@ -368,37 +406,50 @@
     edges0 = send_front(2, kdc3, operand, [(6, pn0)])[:2 * p]
     keep[...] = edges0
     norms_ref[0:1, :] = sums[6:7]
-    for rows in pieces():
+    def sweep_4(rows, carry):
         value = y0[rows, :] - dot(rxt3[rows, :], operand)
         y0[rows, :] = value
         x_h[rows, :], x_l[rows, :] = split(value)
+        return carry
+
+    sweep(sweep_4)
     apply(dual_h, dual_l, q0)
     pass_sums(2)
     e_h, e_l = take_edges(2)
     bend0 = jnp.zeros((1, r), f32)
-    for rows in pieces():
+    def sweep_5(rows, carry):
+        bend0, = carry
         q = q0[rows, :]
         bend0 = bend0 + column_sum(y0[rows, :] * q)
         image = q + spread(rows, e_h, e_l)
         im0[rows, :] = image
         x_h[rows, :], x_l[rows, :] = split(weight[rows, :] * image)
+        return (bend0,)
+
+    bend0, = sweep(sweep_5, (bend0,))
     front(kp_h, kp_l)
     sums = take_sums(2)
     pn0_sum = sums[6:7]
     operand = correction_operand(sums)
 
     send_front(3, kpc3, operand, [(6, bend0)])
-    for rows in pieces():
+    def sweep_6(rows, carry):
         proj = im0[rows, :] - dot(rxt3[rows, :], operand)
         g0[rows, :] = proj
         x_h[rows, :], x_l[rows, :] = split(weight[rows, :] * proj)
+        return carry
+
+    sweep(sweep_6)
     apply(pre_h, pre_l, tq)
     pass_sums(3)
     e_h, e_l = take_edges(3)
-    for rows in pieces():
+    def sweep_7(rows, carry):
         smooth = weight[rows, :] * (tq[rows, :] + spread(rows, e_h, e_l))
         y1[rows, :] = smooth
         x_h[rows, :], x_l[rows, :] = split(smooth)
+        return carry
+
+    sweep(sweep_7)
     front(kd_h, kd_l)
     apply(dual_h, dual_l, gap)
     sums = take_sums(3)
@@ -409,7 +460,8 @@
     send_edges(4, keep[...] - step0 * (out_k[0:2 * p] - dot(kdc3[0:2 * p], operand)))
     zero = jnp.zeros((1, r), f32)
     pn1, norm1, own, cross = zero, zero, zero, zero
-    for rows in pieces():
+    def sweep_8(rows, carry):
+        pn1, norm1, own, cross = carry
         w, old_y, old_q, image = weight[rows, :], y0[rows, :], q0[rows, :], im0[rows, :]
         res = r0[rows, :] - step0 * image
         r0[rows, :] = res
@@ -422,10 +474,16 @@
         tq[rows, :] = q
         own = own + column_sum(value * q)
         cross = cross + column_sum(old_y * q + value * old_q)
+        return (pn1, norm1, own, cross)
+
+    pn1, norm1, own, cross = sweep(sweep_8, (pn1, norm1, own, cross))
     send_sums(4, jnp.zeros((BLOCK, r), f32), [(6, pn1), (7, norm1), (14, own), (15, cross)])
     e_h, e_l = take_edges(4)
-    for rows in pieces():
+    def sweep_9(rows, carry):
         tq[rows, :] = tq[rows, :] + spread(rows, e_h, e_l)
+        return carry
+
+    sweep(sweep_9)
     pass_sums(4)
     sums = take_sums(4)
     pn1_sum = sums[6:7]
@@ -433,9 +491,12 @@
     beta = pn1_sum / pn0_sum
     step1 = pn1_sum / (sums[14:15] + beta * sums[15:16] + beta * beta * bend0_sum)
     on_first = step0 + step1 * beta
-    for rows in pieces():
+    def sweep_10(rows, carry):
         mult_ref[rows, :] = on_first * y0[rows, :] + step1 * y1[rows, :]
         res_ref[rows, :] = r0[rows, :] - step1 * (tq[rows, :] + beta * im0[rows, :])
+        return carry
+
+    sweep(sweep_10)
 
     for side in range(2):
         @pl.when(has[side])
@@ -448,15 +509,6 @@
     for phase in range(PHASES):
         wait_send(one_in.at[phase, pl.ds(0, subs - 1)], one_ss.at[phase])
         wait_send(two_in.at[phase, pl.ds(0, 2 * clusters - 1)], two_ss.at[phase])
-
-
-def write_out(a, b, c, a_out, b_out, c_out, sem):
-    copies = [pltpu.make_async_copy(src, dst, sem.at[at])
-              for at, (src, dst) in enumerate(((a, a_out), (b, b_out), (c, c_out)))]
-    for copy in copies:
-        copy.start()
-    for copy in copies:
-        copy.wait()
 
 
 def solution(mesh):
@@ -474,7 +526,7 @@
         sems = pltpu.SemaphoreType.DMA
         any_spec = pl.BlockSpec(memory_space=pl.ANY)
         vmem_spec = pl.BlockSpec(memory_space=pltpu.VMEM)
-        held = pl.pallas_call(
+        return pl.pallas_call(
             functools.partial(kernel, clusters, subs),
             out_shape=(field, field, pltpu.VMEM((2, r), f32)),
             in_specs=[any_spec, any_spec, vmem_spec, vmem_spec, any_spec, vmem_spec],
@@ -506,13 +558,6 @@
             compiler_params=pltpu.CompilerParams(
                 collective_id=0, has_side_effects=True, vmem_limit_bytes=58 * 1024 * 1024),
         )(dual_ops, boundary_solve_blocks, rigid_images, coarse_rows, gap_raw, row_maps)
-        return pl.pallas_call(
-            write_out,
-            out_shape=tuple(jax.ShapeDtypeStruct(h.shape, h.dtype) for h in held),
-            in_specs=[vmem_spec] * 3,
-            out_specs=(any_spec,) * 3,
-            scratch_shapes=[sems((3,))],
-        )(*held)
 
     rows = P(("cluster", "sub"), None)
     return jax.shard_map(

time: 73.1 us -> 73.6 us (level)
  Pallas kernels: 69.5 us -> 70.3 us
    pallas_call x1, Pallas kernels: 66.6 us -> 70.3 us  [shards(): pl.pallas_call(functools.partial(kernel, clusters, subs), out_shape=(fiel...]
    pallas_call x1 -> x0, Pallas kernels: 2.88 us -> none  [shards(): pl.pallas_call(write_out, out_shape=tuple((jax.ShapeDtypeStruct(h.shape,...]
    unnamed x6 -> x3, local copies, waits for them, and re-layouts: 2.55 us -> 2.52 us
where the time goes in v3:
time: 73.6 us; the launch traced here: 73.4 us
  Pallas kernels  70.3 us (96%)
  local copies, waits for them, and re-layouts  2.52 us (3%)
    pallas_call x1, Pallas kernels, shards(): pl.pallas_call(functools.partial(kernel, clusters, subs), out_shape=(fiel...  70.3 us
    unnamed x3, local copies, waits for them, and re-layouts  2.52 us

profile of v3, /device:TPU:0, one launch (start us, length us, event | category | flops | bytes accessed | tf_op | source)
XLA Modules:
  0.0 73.4 jit_solution(16259851064356995769)
XLA Ops:
  0.6 70.3 %shard_map.85 = (f32[1024,256]{1,0:T(8,128)S(1)}, f32[1024,256]{1,0:T(8,128)S(1)}, f32[2,256]{1,0:T(2,128)S(1)}) custom-call(f32[1024,1024]{1,0:T(8,128)} %dual_hbm.1, f32[1024,1024]{1,0:T(8,128)} %pre_hbm.1, f32[6,1024]{1,0:T(8,128)} %rigid_ref.1, f32[6,192]{1,0:T(8,128)} %coarse_ref.1, f32[1024,256]{1,0:T(8,128)} %gap_hbm.1, s32[1,2,128]{2,1,0:T(2,128)} %maps_ref.1), custom_call_target="tpu_custom_call" | custom-call | tf_op jit(solution)/shard_map/pallas_call | solution.py:529
  70.9 1.0 %copy.12 = f32[1024,256]{1,0:T(8,128)} copy(f32[1024,256]{1,0:T(8,128)S(1)} %get-tuple-element.3) | data formatting | bytes 2097152
  71.9 0.6 copy.14
  72.5 1.0 %copy.13 = f32[1024,256]{1,0:T(8,128)} copy(f32[1024,256]{1,0:T(8,128)S(1)} %get-tuple-element.4) | data formatting | bytes 2097152

commit v4 on v2

--- a/solution.py
+++ b/solution.py
@@ -251,8 +251,10 @@
         c_h, c_l = split(dot3(k_h[...], k_l[...], t_h, t_l))
         kc3[...] = jnp.concatenate([c_h, c_h, c_l], axis=1)
 
-    def apply(high, low, target):
-        target[...] = dot(high[...], x_h[...]) + dot(high[...], x_l[...]) + dot(low[...], x_h[...])
+    first, second = slice(0, m // 2), slice(m // 2, m)
+
+    def apply(high, low, target, rows):
+        target[rows, :] = dot3(high[rows, :], low[rows, :], x_h[...], x_l[...])
 
     def spread(rows, e_h, e_l):
         return dot(place[rows, :], e_h) + dot(place[rows, :], e_l)
@@ -296,6 +298,7 @@
     for i in range(1, clusters):
         remote(mine, mine, co_ss.at[1], co_rs.at[1], (cluster_peer(i), s)).start()
 
+    load_operator(loads[2], dual_in, dual_h, dual_l)
     rw = rx[...] * row_weight
     for source, target in ((rx[...], rxt3), (rw, rxw3)):
         t_h, t_l = split(jnp.transpose(source))
@@ -304,16 +307,15 @@
 
     columns = subs * BLOCK
     i = lax.broadcasted_iota(jnp.int32, (wide, columns), 0)
-    j = lax.broadcasted_iota(jnp.int32, (wide, columns), 1)
+    j = lax.broadcasted_iota(jnp.int32, (1, columns), 1)
+    j_in = lax.rem(j, BLOCK)
     j_mode = lax.rem(j, GROUP)
-    source = (c * subs + lax.div(j, BLOCK) + lax.div(lax.rem(j, BLOCK), GROUP) - 1) * modes + j_mode
-    hot = jnp.where(
-        jnp.logical_and(jnp.logical_and(i == source, j_mode < modes), i < coarse), 1.0, 0.0
-    ).astype(bf16)
-    shape = (clusters * 2 * BLOCK, columns)
-    row = lax.rem(lax.broadcasted_iota(jnp.int32, shape, 0), BLOCK)
-    col = lax.rem(lax.broadcasted_iota(jnp.int32, shape, 1), BLOCK)
-    ones = jnp.where(jnp.logical_and(row == col, lax.rem(row, GROUP) >= modes), 1.0, 0.0)
+    source = (c * subs + lax.div(j, BLOCK) + lax.div(j_in, GROUP) - 1) * modes + j_mode
+    source = jnp.where(jnp.logical_and(j_mode < modes, source < coarse), source, -1)
+    hot = jnp.where(i == source, 1.0, 0.0).astype(bf16)
+    carrying = jnp.where(j_mode >= modes, j_in, -1)
+    row = lax.rem(lax.broadcasted_iota(jnp.int32, (clusters * 2 * BLOCK, 1), 0), BLOCK)
+    ones = jnp.where(row == carrying, 1.0, 0.0)
     wait_recv(coarse_all.at[pl.ds(0, (clusters - 1) * subs)], co_rs.at[1])
     for to_c in range(clusters):
         for k in range(2):
@@ -345,14 +347,13 @@
         proj = r0[rows, :] - dot(rxt3[rows, :], operand)
         p0[rows, :] = proj
         x_h[rows, :], x_l[rows, :] = split(weight[rows, :] * proj)
-    apply(pre_h, pre_l, u0)
+    apply(pre_h, pre_l, u0, first)
     pass_sums(1)
-    load_operator(loads[2], dual_in, dual_h, dual_l)
+    apply(pre_h, pre_l, u0, second)
     edge_operator(dual_h, dual_l, (rx_h, rx_l), kd_h, kd_l, kdc3)
-    for at in range(0, m, chunk):
-        rows = slice(at, at + chunk)
-        t_h, t_l = split(dot3(dual_h[rows, :], dual_l[rows, :], rxt3[:, 0:32], rxt3[:, 64:96]))
-        fx3[rows, :] = jnp.concatenate([t_h, t_h, t_l], axis=1)
+    t_h = jnp.transpose(kd_h[2 * p:, :].astype(f32)).astype(bf16)
+    t_l = jnp.transpose(kd_l[2 * p:, :].astype(f32)).astype(bf16)
+    fx3[...] = jnp.concatenate([t_h, t_h, t_l], axis=1)
     e_h, e_l = take_edges(1)
     pn0 = jnp.zeros((1, r), f32)
     for rows in pieces():
@@ -372,8 +373,9 @@
         value = y0[rows, :] - dot(rxt3[rows, :], operand)
         y0[rows, :] = value
         x_h[rows, :], x_l[rows, :] = split(value)
-    apply(dual_h, dual_l, q0)
+    apply(dual_h, dual_l, q0, first)
     pass_sums(2)
+    apply(dual_h, dual_l, q0, second)
     e_h, e_l = take_edges(2)
     bend0 = jnp.zeros((1, r), f32)
     for rows in pieces():
@@ -392,15 +394,17 @@
         proj = im0[rows, :] - dot(rxt3[rows, :], operand)
         g0[rows, :] = proj
         x_h[rows, :], x_l[rows, :] = split(weight[rows, :] * proj)
-    apply(pre_h, pre_l, tq)
+    apply(pre_h, pre_l, tq, first)
     pass_sums(3)
+    apply(pre_h, pre_l, tq, second)
     e_h, e_l = take_edges(3)
     for rows in pieces():
         smooth = weight[rows, :] * (tq[rows, :] + spread(rows, e_h, e_l))
         y1[rows, :] = smooth
         x_h[rows, :], x_l[rows, :] = split(smooth)
     front(kd_h, kd_l)
-    apply(dual_h, dual_l, gap)
+    apply(dual_h, dual_l, gap, first)
+    apply(dual_h, dual_l, gap, second)
     sums = take_sums(3)
     bend0_sum = sums[6:7]
     step0 = pn0_sum / bend0_sum
@@ -450,15 +454,6 @@
         wait_send(two_in.at[phase, pl.ds(0, 2 * clusters - 1)], two_ss.at[phase])
 
 
-def write_out(a, b, c, a_out, b_out, c_out, sem):
-    copies = [pltpu.make_async_copy(src, dst, sem.at[at])
-              for at, (src, dst) in enumerate(((a, a_out), (b, b_out), (c, c_out)))]
-    for copy in copies:
-        copy.start()
-    for copy in copies:
-        copy.wait()
-
-
 def solution(mesh):
     clusters, subs = mesh.shape["cluster"], mesh.shape["sub"]
 
@@ -474,7 +469,7 @@
         sems = pltpu.SemaphoreType.DMA
         any_spec = pl.BlockSpec(memory_space=pl.ANY)
         vmem_spec = pl.BlockSpec(memory_space=pltpu.VMEM)
-        held = pl.pallas_call(
+        return pl.pallas_call(
             functools.partial(kernel, clusters, subs),
             out_shape=(field, field, pltpu.VMEM((2, r), f32)),
             in_specs=[any_spec, any_spec, vmem_spec, vmem_spec, any_spec, vmem_spec],
@@ -506,13 +501,6 @@
             compiler_params=pltpu.CompilerParams(
                 collective_id=0, has_side_effects=True, vmem_limit_bytes=58 * 1024 * 1024),
         )(dual_ops, boundary_solve_blocks, rigid_images, coarse_rows, gap_raw, row_maps)
-        return pl.pallas_call(
-            write_out,
-            out_shape=tuple(jax.ShapeDtypeStruct(h.shape, h.dtype) for h in held),
-            in_specs=[vmem_spec] * 3,
-            out_specs=(any_spec,) * 3,
-            scratch_shapes=[sems((3,))],
-        )(*held)
 
     rows = P(("cluster", "sub"), None)
     return jax.shard_map(

time: 73.1 us -> 66.9 us (0.915)
  Pallas kernels: 69.5 us -> 63.5 us
    pallas_call x1, Pallas kernels: 66.6 us -> 63.5 us  [shards(): pl.pallas_call(functools.partial(kernel, clusters, subs), out_shape=(fiel...]
    pallas_call x1 -> x0, Pallas kernels: 2.88 us -> none  [shards(): pl.pallas_call(write_out, out_shape=tuple((jax.ShapeDtypeStruct(h.shape,...]
    unnamed x6 -> x3, local copies, waits for them, and re-layouts: 2.55 us -> 2.52 us
where the time goes in v4:
time: 66.9 us; the launch traced here: 66.7 us
  Pallas kernels  63.5 us (95%)
  local copies, waits for them, and re-layouts  2.52 us (4%)
    pallas_call x1, Pallas kernels, shards(): pl.pallas_call(functools.partial(kernel, clusters, subs), out_shape=(fiel...  63.5 us
    unnamed x3, local copies, waits for them, and re-layouts  2.52 us

profile of v4, /device:TPU:0, one launch (start us, length us, event | category | flops | bytes accessed | tf_op | source)
XLA Modules:
  0.0 66.7 jit_solution(10952359376513315462)
XLA Ops:
  0.6 63.5 %shard_map.85 = (f32[1024,256]{1,0:T(8,128)S(1)}, f32[1024,256]{1,0:T(8,128)S(1)}, f32[2,256]{1,0:T(2,128)S(1)}) custom-call(f32[1024,1024]{1,0:T(8,128)} %dual_hbm.1, f32[1024,1024]{1,0:T(8,128)} %pre_hbm.1, f32[6,1024]{1,0:T(8,128)} %rigid_ref.1, f32[6,192]{1,0:T(8,128)} %coarse_ref.1, f32[1024,256]{1,0:T(8,128)} %gap_hbm.1, s32[1,2,128]{2,1,0:T(2,128)} %maps_ref.1), custom_call_target="tpu_custom_call" | custom-call | tf_op jit(solution)/shard_map/pallas_call | solution.py:472
  64.2 1.0 %copy.12 = f32[1024,256]{1,0:T(8,128)} copy(f32[1024,256]{1,0:T(8,128)S(1)} %get-tuple-element.3) | data formatting | bytes 2097152
  65.1 0.6 copy.14
  65.7 1.0 %copy.13 = f32[1024,256]{1,0:T(8,128)} copy(f32[1024,256]{1,0:T(8,128)S(1)} %get-tuple-element.4) | data formatting | bytes 2097152

commit v5 on v4

--- a/solution.py
+++ b/solution.py
@@ -42,8 +42,9 @@
            gap, place, pick, weight, rx, rxt3, rxw3, fx3, kpc3, kdc3, out_k, keep, x_h, x_l,
            q0,
            coarse_all, coarse_pick, mix_h, mix_l, rig_out, rig_in,
-           one_out, one_in, two_out, two_in, ex_out, ex_in,
-           load_sem, rig_ss, rig_rs, co_ss, co_rs, one_ss, one_rs, two_ss, two_rs, ex_ss, ex_rs):
+           one_out, one_in, two_out, two_in, last_one, last_two, ex_out, ex_in,
+           load_sem, rig_ss, rig_rs, co_ss, co_rs, one_ss, one_rs, two_ss, two_rs,
+           last_ss, last_rs, ex_ss, ex_rs):
     total = clusters * subs
     modes, m = rigid_ref.shape
     coarse = coarse_ref.shape[1]
@@ -348,8 +349,8 @@
         p0[rows, :] = proj
         x_h[rows, :], x_l[rows, :] = split(weight[rows, :] * proj)
     apply(pre_h, pre_l, u0, first)
+    apply(pre_h, pre_l, u0, second)
     pass_sums(1)
-    apply(pre_h, pre_l, u0, second)
     edge_operator(dual_h, dual_l, (rx_h, rx_l), kd_h, kd_l, kdc3)
     t_h = jnp.transpose(kd_h[2 * p:, :].astype(f32)).astype(bf16)
     t_l = jnp.transpose(kd_l[2 * p:, :].astype(f32)).astype(bf16)
@@ -426,16 +427,30 @@
         tq[rows, :] = q
         own = own + column_sum(value * q)
         cross = cross + column_sum(old_y * q + value * old_q)
-    send_sums(4, jnp.zeros((BLOCK, r), f32), [(6, pn1), (7, norm1), (14, own), (15, cross)])
+    parts = (pn1, norm1, own, cross)
+    last_one[s] = jnp.concatenate(
+        [part[:, k * HALF:(k + 1) * HALF] for k in range(2) for part in parts], axis=0)
+
+    def last_sub(i):
+        remote(last_one.at[s], last_one.at[s], last_ss.at[0], last_rs.at[0],
+               (c, sub_peer(i))).start()
+
+    each(1, subs, last_sub)
     e_h, e_l = take_edges(4)
     for rows in pieces():
         tq[rows, :] = tq[rows, :] + spread(rows, e_h, e_l)
-    pass_sums(4)
-    sums = take_sums(4)
-    pn1_sum = sums[6:7]
-    norms_ref[1:2, :] = sums[7:8]
+    wait_recv(last_one.at[pl.ds(0, subs - 1)], last_rs.at[0])
+    last_two[c] = jnp.sum(last_one[...], axis=0)
+    for i in range(1, clusters):
+        remote(last_two.at[c], last_two.at[c], last_ss.at[1], last_rs.at[1],
+               (cluster_peer(i), s)).start()
+    wait_recv(last_two.at[pl.ds(0, clusters - 1)], last_rs.at[1])
+    halves = jnp.sum(last_two[...], axis=0)
+    sums = jnp.concatenate([halves[0:4], halves[4:8]], axis=1)
+    pn1_sum = sums[0:1]
+    norms_ref[1:2, :] = sums[1:2]
     beta = pn1_sum / pn0_sum
-    step1 = pn1_sum / (sums[14:15] + beta * sums[15:16] + beta * beta * bend0_sum)
+    step1 = pn1_sum / (sums[2:3] + beta * sums[3:4] + beta * beta * bend0_sum)
     on_first = step0 + step1 * beta
     for rows in pieces():
         mult_ref[rows, :] = on_first * y0[rows, :] + step1 * y1[rows, :]
@@ -449,7 +464,9 @@
                 ex_copy(phase, side).wait_send()
     wait_send(coarse_all.at[pl.ds(0, subs - 1)], co_ss.at[0])
     wait_send(coarse_all.at[pl.ds(0, (clusters - 1) * subs)], co_ss.at[1])
-    for phase in range(PHASES):
+    wait_send(last_one.at[pl.ds(0, subs - 1)], last_ss.at[0])
+    wait_send(last_two.at[pl.ds(0, clusters - 1)], last_ss.at[1])
+    for phase in range(PHASES - 1):
         wait_send(one_in.at[phase, pl.ds(0, subs - 1)], one_ss.at[phase])
         wait_send(two_in.at[phase, pl.ds(0, 2 * clusters - 1)], two_ss.at[phase])
 
@@ -488,14 +505,16 @@
                 pltpu.VMEM((clusters * 2 * BLOCK, wide), f32),
                 mix16, mix16,
                 pltpu.VMEM((2, GROUP, p), f32), pltpu.VMEM((2, GROUP, p), f32),
-                pltpu.VMEM((PHASES, 2, BLOCK, HALF), f32),
-                pltpu.VMEM((PHASES, subs, BLOCK, HALF), f32),
-                pltpu.VMEM((PHASES, 2 * clusters, BLOCK, HALF), f32),
-                pltpu.VMEM((PHASES, 2 * clusters, BLOCK, HALF), f32),
+                pltpu.VMEM((PHASES - 1, 2, BLOCK, HALF), f32),
+                pltpu.VMEM((PHASES - 1, subs, BLOCK, HALF), f32),
+                pltpu.VMEM((PHASES - 1, 2 * clusters, BLOCK, HALF), f32),
+                pltpu.VMEM((PHASES - 1, 2 * clusters, BLOCK, HALF), f32),
+                pltpu.VMEM((subs, GROUP, HALF), f32), pltpu.VMEM((clusters, GROUP, HALF), f32),
                 pltpu.VMEM((PHASES, 2, p, r), f32),
                 pltpu.VMEM((PHASES, 2, p, r), f32),
                 sems((3,)), sems((2,)), sems((2,)), sems((2,)), sems((2,)),
-                sems((PHASES,)), sems((PHASES,)), sems((PHASES,)), sems((PHASES,)),
+                sems((PHASES - 1,)), sems((PHASES - 1,)), sems((PHASES - 1,)), sems((PHASES - 1,)),
+                sems((2,)), sems((2,)),
                 sems((PHASES, 2)), sems((PHASES, 2)),
             ],
             compiler_params=pltpu.CompilerParams(

time: 66.9 us -> 65 us (0.972)
  Pallas kernels: 63.5 us -> 61.6 us
    pallas_call x1, Pallas kernels: 63.5 us -> 61.6 us  [shards(): pl.pallas_call(functools.partial(kernel, clusters, subs), out_shape=(fiel...]
where the time goes in v5:
time: 65 us; the launch traced here: 64.8 us
  Pallas kernels  61.6 us (95%)
  local copies, waits for them, and re-layouts  2.52 us (4%)
    pallas_call x1, Pallas kernels, shards(): pl.pallas_call(functools.partial(kernel, clusters, subs), out_shape=(fiel...  61.6 us
    unnamed x3, local copies, waits for them, and re-layouts  2.52 us

profile of v5, /device:TPU:0, one launch (start us, length us, event | category | flops | bytes accessed | tf_op | source)
XLA Modules:
  0.0 64.8 jit_solution(15803395530709105789)
XLA Ops:
  0.6 61.6 %shard_map.85 = (f32[1024,256]{1,0:T(8,128)S(1)}, f32[1024,256]{1,0:T(8,128)S(1)}, f32[2,256]{1,0:T(2,128)S(1)}) custom-call(f32[1024,1024]{1,0:T(8,128)} %dual_hbm.1, f32[1024,1024]{1,0:T(8,128)} %pre_hbm.1, f32[6,1024]{1,0:T(8,128)} %rigid_ref.1, f32[6,192]{1,0:T(8,128)} %coarse_ref.1, f32[1024,256]{1,0:T(8,128)} %gap_hbm.1, s32[1,2,128]{2,1,0:T(2,128)} %maps_ref.1), custom_call_target="tpu_custom_call" | custom-call | tf_op jit(solution)/shard_map/pallas_call | solution.py:489
  62.3 1.0 %copy.12 = f32[1024,256]{1,0:T(8,128)} copy(f32[1024,256]{1,0:T(8,128)S(1)} %get-tuple-element.3) | data formatting | bytes 2097152
  63.2 0.6 copy.14
  63.8 1.0 %copy.13 = f32[1024,256]{1,0:T(8,128)} copy(f32[1024,256]{1,0:T(8,128)S(1)} %get-tuple-element.4) | data formatting | bytes 2097152

commit v6 on v5

--- a/solution.py
+++ b/solution.py
@@ -26,6 +26,11 @@
 
 def dot3(a_high, a_low, b_high, b_low):
     return dot(a_high, b_high) + dot(a_high, b_low) + dot(a_low, b_high)
+
+
+def stacked3(a_high, a_low, b_high, b_low):
+    return dot(jnp.concatenate([a_high, a_high, a_low], axis=1),
+               jnp.concatenate([b_high, b_low, b_high], axis=0))
 
 
 def each(low, high, body):
@@ -255,10 +260,10 @@
     first, second = slice(0, m // 2), slice(m // 2, m)
 
     def apply(high, low, target, rows):
-        target[rows, :] = dot3(high[rows, :], low[rows, :], x_h[...], x_l[...])
+        target[rows, :] = stacked3(high[rows, :], low[rows, :], x_h[...], x_l[...])
 
     def spread(rows, e_h, e_l):
-        return dot(place[rows, :], e_h) + dot(place[rows, :], e_l)
+        return dot(jnp.concatenate([place[rows, :]] * 2, axis=1), jnp.concatenate([e_h, e_l], axis=0))
 
     def pieces():
         return [slice(at, at + chunk) for at in range(0, m, chunk)]
@@ -267,7 +272,7 @@
         return jnp.sum(x, axis=0, keepdims=True)
 
     def front(k_h, k_l):
-        out_k[...] = dot3(k_h[...], k_l[...], x_h[...], x_l[...])
+        out_k[...] = stacked3(k_h[...], k_l[...], x_h[...], x_l[...])
 
     def send_front(phase, kc3, operand, sums):
         out = out_k[...] - dot(kc3[...], operand)

time: 65 us -> 64.8 us (level)
  no operation moved by 1% of the time
where the time goes in v6:
time: 64.8 us; the launch traced here: 64.7 us
  Pallas kernels  61.5 us (95%)
  local copies, waits for them, and re-layouts  2.52 us (4%)
    pallas_call x1, Pallas kernels, shards(): pl.pallas_call(functools.partial(kernel, clusters, subs), out_shape=(fiel...  61.5 us
    unnamed x3, local copies, waits for them, and re-layouts  2.52 us

profile of v6, /device:TPU:0, one launch (start us, length us, event | category | flops | bytes accessed | tf_op | source)
XLA Modules:
  0.0 64.7 jit_solution(17517329154623738078)
XLA Ops:
  0.6 61.5 %shard_map.85 = (f32[1024,256]{1,0:T(8,128)S(1)}, f32[1024,256]{1,0:T(8,128)S(1)}, f32[2,256]{1,0:T(2,128)S(1)}) custom-call(f32[1024,1024]{1,0:T(8,128)} %dual_hbm.1, f32[1024,1024]{1,0:T(8,128)} %pre_hbm.1, f32[6,1024]{1,0:T(8,128)} %rigid_ref.1, f32[6,192]{1,0:T(8,128)} %coarse_ref.1, f32[1024,256]{1,0:T(8,128)} %gap_hbm.1, s32[1,2,128]{2,1,0:T(2,128)} %maps_ref.1), custom_call_target="tpu_custom_call" | custom-call | tf_op jit(solution)/shard_map/pallas_call | solution.py:494
  62.1 1.0 %copy.12 = f32[1024,256]{1,0:T(8,128)} copy(f32[1024,256]{1,0:T(8,128)S(1)} %get-tuple-element.3) | data formatting | bytes 2097152
  63.1 0.6 copy.14
  63.7 1.0 %copy.13 = f32[1024,256]{1,0:T(8,128)} copy(f32[1024,256]{1,0:T(8,128)S(1)} %get-tuple-element.4) | data formatting | bytes 2097152
